TPU v7x, 128 devices: a whole 4x4x4 slice. The times are simulated.
128 devices in a mesh: bis: 16 (over y, z), dom: 8 (over x, core).
Axes of the slice: x: 4, y: 4, z: 4, core: 2. Of those that a mesh axis runs over, the one named last changes fastest.
Arguments:
- positions: float32 [16, 256, 3, 128], P('bis', 'dom'), may hold values from 0 to 1
- velocities: float32 [16, 256, 3, 128], P('bis', 'dom'), may hold values from -3 to 3
- radii: float32 [16, 256, 128], P('bis', 'dom'), may hold values from 0.05 to 0.12
- drag_rates: float32 [16, 256, 128], P('bis', 'dom'), may hold values from 1 to 6
- mig_slots: int32 [16, 24, 16], P('bis', 'dom'), may hold values from 0 to 31, as said below
- mig_counts: int32 [16, 24], P('bis', 'dom'), may hold values from 1 to 16, as said below
- pair_lists: int32 [16, 2, 1536], P('bis', None, 'dom'), may hold values from 0 to 39, as said below
- pair_counts: int32 [16, 8], P('bis', 'dom'), may hold values from 48 to 192, as said below
- owners: int32 [16, 256], P('bis', 'dom'), may hold values from 0 to 2047
- dep_weights: bfloat16 [16, 256, 128, 128], P('bis', 'dom'), may hold values from 0 to 0.015625
- fluid_velocity: float32 [8, 2048, 3, 128], P('dom', 'bis'), may hold values from -6 to 6
Outputs:
- positions_out: float32 [16, 256, 3, 128], P('bis', 'dom')
- velocities_out: float32 [16, 256, 3, 128], P('bis', 'dom')
- fluid_out: float32 [8, 2048, 3, 128], P('dom', 'bis')
- voidage: float32 [8, 2048, 128], P('dom', 'bis')
Inputs may be any that keep to these rules, and one draw needn't show every extreme that they name: `mig_slots`: within one device and level the 16 slots are distinct block indices. `mig_counts`: at level l the two devices whose bis indices differ only in bit l, at the same dom index, have equal counts; some such pair has exactly 16. `pair_lists`: row 0 holds blocks below 32; row 1 indexes the 40 extended blocks; entries past a device's count are unused. `pair_counts`: each count is 192 divided by 1, 2, 3 or 4, rounded down; some device has exactly 192.
All inputs are finite; a program needn't handle non-finite values.
Results may differ from a plain program's by a relative error of at most 0.0003.
Values may be sent and summed in bfloat16 or wider, within the bound.
A program may use at most 64 MiB of HBM per device.

v0:
```python
import jax
import jax.numpy as jnp
from jax import lax
from jax.sharding import PartitionSpec as P

G = 4
SUBSTEPS = 2
PAIR_BATCH = 16


STIFFNESS = 5.0
DAMPING = 1.0
TIME_STEP = 0.05
EPS_DIST = 0.0001
RADIUS_REF = 0.1
FLUID_GAIN = 0.2


def from_partner(value, axis, stride):
    mask = 2**stride
    pairs = [(source, source ^ mask) for source in range(lax.axis_size(axis))]
    return lax.ppermute(value, axis, pairs)


def with_halo(block, sides, width):
    for axis, dim in sides:
        count = lax.axis_size(axis)
        forward = [(i, i + 1) for i in range(count - 1)]
        forward.append((count - 1, 0))
        backward = [(target, source) for source, target in forward]
        low = lax.ppermute(
            lax.slice_in_dim(block, block.shape[dim] - width, None, axis=dim), axis, forward
        )
        high = lax.ppermute(lax.slice_in_dim(block, 0, width, axis=dim), axis, backward)
        block = jnp.concatenate([low, block, high], axis=dim)
    return block


def pair_forces(left_blk, right_blk):
    offset = left_blk[:, 0:3, :, None] - right_blk[:, 0:3, None, :]
    distance = jnp.sqrt(jnp.sum(offset * offset, axis=1) + EPS_DIST)
    intersection = jnp.maximum(left_blk[:, 6, :, None] + right_blk[:, 6, None, :] - distance, 0.0)
    rel_vel = left_blk[:, 3:6, :, None] - right_blk[:, 3:6, None, :]
    normal_speed = jnp.sum(rel_vel * offset, axis=1) / distance
    factor = intersection * (STIFFNESS - DAMPING * normal_speed) / distance
    return jnp.sum(factor[:, None] * offset, axis=3)


def contact_forces(padded, left_ids, right_ids, pair_total, batches):
    blocks = padded.shape[0] - 2 * G
    empty_sum = jnp.zeros((blocks, 3 * padded.shape[2]), jnp.float32)

    def accumulate(batch_idx, summed):
        first_row = batch_idx * PAIR_BATCH
        left = lax.dynamic_slice_in_dim(left_ids, first_row, PAIR_BATCH)
        right = lax.dynamic_slice_in_dim(right_ids, first_row, PAIR_BATCH)
        is_live = first_row + jnp.arange(PAIR_BATCH, dtype=jnp.int32) < pair_total
        forces = pair_forces(padded[left + G], padded[right])
        forces = jnp.where(is_live[:, None, None], forces, 0.0)
        onehot = (jnp.arange(blocks, dtype=jnp.int32)[:, None] == left[None, :]).astype(jnp.float32)
        return summed + jnp.dot(
            onehot, forces.reshape(PAIR_BATCH, -1), precision=lax.Precision.HIGHEST
        )

    return lax.fori_loop(0, batches, accumulate, empty_sum)


def local(
    positions,
    velocities,
    radii,
    drag_rates,
    mig_slots,
    mig_counts,
    pair_lists,
    pair_counts,
    owners,
    dep_weights,
    fluid_velocity,
):
    particle_state = jnp.concatenate(
        [positions[0], velocities[0], radii[0][:, None], drag_rates[0][:, None]], axis=1
    )
    blocks = particle_state.shape[0]
    blk_width = particle_state.shape[2]
    capacity = mig_slots.shape[2]
    slot_idx = jnp.arange(capacity, dtype=jnp.int32)
    for bit_level in range(mig_slots.shape[1]):
        slot_list = mig_slots[0, bit_level]
        outgoing = particle_state[slot_list]
        incoming = from_partner(outgoing, "bis", bit_level)
        is_live = slot_idx < mig_counts[0, bit_level]
        chosen = jnp.where(is_live[:, None, None], incoming, outgoing)
        particle_state = particle_state.at[slot_list].set(chosen)
    fb_dev = fluid_velocity.shape[1]
    cells = fluid_velocity.shape[3]
    fluid_bf = fluid_velocity[0].astype(jnp.bfloat16).reshape(fb_dev, 3 * cells)
    owner_map = owners[0]
    weights = dep_weights[0]
    shard_piece = lax.all_gather(fluid_bf, "bis", axis=0, tiled=True)
    onehot = (
        owner_map[:, None] == jnp.arange(shard_piece.shape[0], dtype=jnp.int32)[None, :]
    ).astype(jnp.bfloat16)
    carried = jnp.dot(onehot, shard_piece, preferred_element_type=jnp.float32)
    fluid_blk = carried.astype(jnp.bfloat16).reshape(blocks, 3, cells)
    sampled = jnp.einsum("npc,nkc->nkp", weights, fluid_blk, preferred_element_type=jnp.float32)
    left_ids = pair_lists[0, 0]
    right_ids = pair_lists[0, 1]
    pair_total = pair_counts[0, 0]
    for substep in range(SUBSTEPS):
        padded = with_halo(particle_state, (("dom", 0),), G)
        contact = contact_forces(
            padded, left_ids, right_ids, pair_total, left_ids.shape[0] // PAIR_BATCH
        )
        contact = contact.reshape(blocks, 3, blk_width)
        masses = (particle_state[:, 6] / RADIUS_REF) ** 3
        beta = particle_state[:, 7]
        velocity = particle_state[:, 3:6]
        velocity = velocity + TIME_STEP * (
            contact / masses[:, None] + beta[:, None] * (sampled - velocity)
        )
        position = particle_state[:, 0:3] + TIME_STEP * velocity
        particle_state = jnp.concatenate([position, velocity, particle_state[:, 6:8]], axis=1)
    masses = (particle_state[:, 6] / RADIUS_REF) ** 3
    beta = particle_state[:, 7]
    velocity = particle_state[:, 3:6]
    payload = jnp.concatenate(
        [(masses * beta)[:, None] * (sampled - velocity), masses[:, None]], axis=1
    ).astype(jnp.bfloat16)
    deposits = jnp.einsum(
        "nkp,npc->nkc", payload, weights, preferred_element_type=jnp.float32
    ).reshape(blocks, 4 * cells)
    fluid_rows = jnp.arange(fb_dev * lax.axis_size("bis"), dtype=jnp.int32)
    onehot = (fluid_rows[:, None] == owner_map[None, :]).astype(jnp.float32)
    totals = lax.psum_scatter(
        jnp.dot(onehot, deposits, precision=lax.Precision.HIGHEST),
        "bis",
        scatter_dimension=0,
        tiled=True,
    )
    totals = totals.reshape(fb_dev, 4, cells)
    solid = totals[:, 3]
    voidage = 1.0 / (1.0 + solid)
    fluid_out = fluid_velocity[0] - FLUID_GAIN * totals[:, 0:3] / (1.0 + solid)[:, None]
    return (
        particle_state[None, :, 0:3],
        particle_state[None, :, 3:6],
        fluid_out[None],
        voidage[None],
    )


def solution(mesh):
    in_specs = (
        P("bis", "dom", None, None),
        P("bis", "dom", None, None),
        P("bis", "dom", None),
        P("bis", "dom", None),
        P("bis", "dom", None),
        P("bis", "dom"),
        P("bis", None, "dom"),
        P("bis", "dom"),
        P("bis", "dom"),
        P("bis", "dom", None, None),
        P("dom", "bis", None, None),
    )
    out_specs = (
        P("bis", "dom", None, None),
        P("bis", "dom", None, None),
        P("dom", "bis", None, None),
        P("dom", "bis", None),
    )
    return jax.shard_map(local, mesh=mesh, in_specs=in_specs, out_specs=out_specs, check_vma=False)
```

profile of v0, /device:TPU:0, one launch (start us, length us, event | category | flops | bytes accessed | tf_op | source)
XLA Modules:
  0.0 301.2 jit_solution(15563618511348249601)
XLA Ops:
  7.2 1.8 copy.30
  12.0 2.1 collective-permute-start
  14.1 1.4 fusion.41
  18.6 3.7 %collective-permute-start.1 = (f32[16,8,128]{2,1,0:T(8,128)S(1)}, f32[16,8,128]{2,1,0:T(8,128)S(1)}, u32[]{:S(2)}, u32[]{:S(2)}) collective-permute-start(f32[16,8,128]{2,1,0:T(8,128)S(1)} %gather_fusion.5), channel_id=1, source_target_pairs={{0,16},{8,24},{16,0},{24,8},{32,48},{40,56},{48,32},{56,40},{64,80... | collective-permute-start | bytes 196616 | tf_op jit(solution)/shard_map/ppermute | solution.py:22
  22.9 1.7 collective-permute-done.1
  26.3 1.7 collective-permute-start.2
  28.6 2.1 collective-permute-done.2
  31.9 2.9 collective-permute-start.4
  34.9 1.3 collective-permute-done.3
  36.3 81.9 %while.32 = (s32[]{:T(128)}, f32[32,384]{1,0:T(8,128)S(1)}, s32[192]{0:T(256)S(1)}, s32[]{:T(128)}, f32[40,8,128]{2,1,0:T(8,128)S(1)}, /*index=5*/s32[192]{0:T(256)S(1)}, s32[]{:T(128)}, s32[]{:T(128)}, s32[]{:T(128)}, s32[]{:T(128)}) while((s32[]{:T(128)}, f32[32,384]{1,0:T(8,128)S(1)}, s32[192]{0:T(256)S(1)}, s32[]{:T(128)}, ...), condition=%wide.region_7.8_spmd.clone, body=%wide.region_3.7_spmd.clone.sunk | while | flops 11037335 | bytes 7103313 | solution.py:65
  38.3 2.1 fusion.54
  41.0 1.9 fusion.55
  45.1 2.1 fusion.54
  47.9 1.9 fusion.55
  52.0 2.1 fusion.54
  54.7 1.9 fusion.55
  58.8 2.1 fusion.54
  61.5 1.9 fusion.55
  65.6 2.1 fusion.54
  68.3 1.9 fusion.55
  72.4 2.1 fusion.54
  75.2 1.9 fusion.55
  79.3 2.1 fusion.54
  82.0 1.9 fusion.55
  86.1 2.1 fusion.54
  88.8 1.9 fusion.55
  92.9 2.1 fusion.54
  95.6 1.9 fusion.55
  99.7 2.1 fusion.54
  102.5 1.9 fusion.55
  106.6 2.1 fusion.54
  109.3 1.9 fusion.55
  113.4 2.1 fusion.54
  116.1 1.9 fusion.55
  118.3 2.0 convolution_convert_fusion
  121.4 2.6 collective-permute-start.6
  124.0 1.4 collective-permute-done.5
  125.5 81.8 %while.33 = (s32[]{:T(128)}, f32[32,384]{1,0:T(8,128)S(1)}, s32[192]{0:T(256)S(1)}, s32[]{:T(128)}, f32[40,8,128]{2,1,0:T(8,128)S(1)}, /*index=5*/s32[192]{0:T(256)S(1)}, s32[]{:T(128)}, s32[]{:T(128)}, s32[]{:T(128)}, s32[]{:T(128)}) while((s32[]{:T(128)}, f32[32,384]{1,0:T(8,128)S(1)}, s32[192]{0:T(256)S(1)}, s32[]{:T(128)}, ...), condition=%wide.region_12.13_spmd.clone, body=%wide.region_8.12_spmd.clone.sunk | while | flops 11037335 | bytes 7103313 | solution.py:65
  127.5 2.1 fusion.58
  130.2 1.9 fusion.59
  134.3 2.1 fusion.58
  137.0 1.9 fusion.59
  141.1 2.1 fusion.58
  143.9 1.9 fusion.59
  148.0 2.1 fusion.58
  150.7 1.9 fusion.59
  154.8 2.1 fusion.58
  157.5 1.9 fusion.59
  161.6 2.1 fusion.58
  164.3 1.9 fusion.59
  168.4 2.1 fusion.58
  171.1 1.9 fusion.59
  175.2 2.1 fusion.58
  178.0 1.9 fusion.59
  182.1 2.1 fusion.58
  184.8 1.9 fusion.59
  188.9 2.1 fusion.58
  191.6 1.9 fusion.59
  195.7 2.1 fusion.58
  198.4 1.9 fusion.59
  202.5 2.1 fusion.58
  205.2 1.9 fusion.59
  207.8 3.7 %fusion.20 = f32[2048,512]{1,0:T(8,128)} fusion(s32[32]{0:T(128)S(1)} %bitcast.105, f32[4,8,4,128]{3,2,1,0:T(4,128)S(1)} %bitcast.93), kind=kOutput, calls=%fused_computation.56 | convolution fusion | flops 402718720 | bytes 4259968 | tf_op jit(solution)/shard_map/dot_general | solution.py:136
  212.9 79.0 %reduce-scatter.2.cloned.1.call-done = f32[128,512]{1,0:T(8,128)} async-done(((f32[2048,512]{1,0:T(8,128)}), f32[128,512]{1,0:T(8,128)}) %reduce-scatter.2.cloned.1.call-update) | async-done | bytes 262160 | tf_op jit(solution)/shard_map/reduce_scatter | solution.py:135
  (346 shorter events, 83.0 us)
Async XLA Ops:
  7.2 113.1 %copy-start = (bf16[1,32,128,128]{3,2,1,0:T(8,128)(2,1)S(1)}, bf16[1,32,128,128]{3,2,1,0:T(8,128)(2,1)}, u32[]{:S(2)}) copy-start(bf16[1,32,128,128]{3,2,1,0:T(8,128)(2,1)} %param.24) | copy-start | bytes 3145732
  7.2 111.1 %all-gather.2.cloned.1.call-start = ((), (), s32[]{:S(2)}) async-start(), calls=%async_computation.1 | async-start | bytes 1671168 | tf_op jit(solution)/shard_map/all_gather | solution.py:100
  9.0 282.9 %reduce-scatter.2.cloned.1.call-start = ((), (), s32[]{:S(2)}) async-start(), calls=%async_computation.2 | async-start | bytes 4456448 | tf_op jit(solution)/shard_map/reduce_scatter | solution.py:135
  12.0 4.9 %collective-permute-start = (f32[16,8,128]{2,1,0:T(8,128)S(1)}, f32[16,8,128]{2,1,0:T(8,128)S(1)}, u32[]{:S(2)}, u32[]{:S(2)}) collective-permute-start(f32[16,8,128]{2,1,0:T(8,128)S(1)} %gather_fusion.4), channel_id=1, source_target_pairs={{0,8},{8,0},{16,24},{24,16},{32,40},{40,32},{48,56},{56,48},{64,72... | collective-permute-start | bytes 196616 | tf_op jit(solution)/shard_map/ppermute | solution.py:22
  18.6 6.0 %collective-permute-start.1 = (f32[16,8,128]{2,1,0:T(8,128)S(1)}, f32[16,8,128]{2,1,0:T(8,128)S(1)}, u32[]{:S(2)}, u32[]{:S(2)}) collective-permute-start(f32[16,8,128]{2,1,0:T(8,128)S(1)} %gather_fusion.5), channel_id=1, source_target_pairs={{0,16},{8,24},{16,0},{24,8},{32,48},{40,56},{48,32},{56,40},{64,80... | collective-permute-start | bytes 196616 | tf_op jit(solution)/shard_map/ppermute | solution.py:22
  26.3 4.4 %collective-permute-start.2 = (f32[16,8,128]{2,1,0:T(8,128)S(1)}, f32[16,8,128]{2,1,0:T(8,128)S(1)}, u32[]{:S(2)}, u32[]{:S(2)}) collective-permute-start(f32[16,8,128]{2,1,0:T(8,128)S(1)} %gather_fusion.6), channel_id=1, source_target_pairs={{0,32},{8,40},{16,48},{24,56},{32,0},{40,8},{48,16},{56,24},{64,96... | collective-permute-start | bytes 196616 | tf_op jit(solution)/shard_map/ppermute | solution.py:22
  31.9 4.4 %collective-permute-start.3 = (f32[4,8,128]{2,1,0:T(8,128)S(1)}, f32[4,8,128]{2,1,0:T(8,128)S(1)}, u32[]{:S(2)}, u32[]{:S(2)}) collective-permute-start(f32[4,8,128]{2,1,0:T(8,128)S(1)} %get-tuple-element.419), channel_id=1, source_target_pairs={{0,1},{1,2},{2,3},{3,4},{4,5},{5,6},{6,7},{7,0},{8,9},{9,10},{10,1... | collective-permute-start | bytes 49160 | tf_op jit(solution)/shard_map/ppermute | solution.py:31
  31.9 4.4 %collective-permute-start.4 = (f32[4,8,128]{2,1,0:T(8,128)S(1)}, f32[4,8,128]{2,1,0:T(8,128)S(1)}, u32[]{:S(2)}, u32[]{:S(2)}) collective-permute-start(f32[4,8,128]{2,1,0:T(8,128)S(1)} %get-tuple-element.420), channel_id=1, source_target_pairs={{1,0},{2,1},{3,2},{4,3},{5,4},{6,5},{7,6},{0,7},{9,8},{10,9},{11,1... | collective-permute-start | bytes 49160 | tf_op jit(solution)/shard_map/ppermute | solution.py:34
  36.3 82.0 %copy-start.2 = (s32[1,32]{1,0:T(1,128)S(1)}, s32[1,32]{1,0:T(1,128)}, u32[]{:S(2)}) copy-start(s32[1,32]{1,0:T(1,128)} %param.23) | copy-start | bytes 388
  121.0 4.4 %collective-permute-start.5 = (f32[4,8,128]{2,1,0:T(8,128)S(1)}, f32[4,8,128]{2,1,0:T(8,128)S(1)}, u32[]{:S(2)}, u32[]{:S(2)}) collective-permute-start(f32[4,8,128]{2,1,0:T(8,128)S(1)} %get-tuple-element.416), channel_id=1, source_target_pairs={{0,1},{1,2},{2,3},{3,4},{4,5},{5,6},{6,7},{7,0},{8,9},{9,10},{10,1... | collective-permute-start | bytes 49160 | tf_op jit(solution)/shard_map/ppermute | solution.py:31
  121.4 4.1 %collective-permute-start.6 = (f32[4,8,128]{2,1,0:T(8,128)S(1)}, f32[4,8,128]{2,1,0:T(8,128)S(1)}, u32[]{:S(2)}, u32[]{:S(2)}) collective-permute-start(f32[4,8,128]{2,1,0:T(8,128)S(1)} %get-tuple-element.417), channel_id=1, source_target_pairs={{1,0},{2,1},{3,2},{4,3},{5,4},{6,5},{7,6},{0,7},{9,8},{10,9},{11,1... | collective-permute-start | bytes 49160 | tf_op jit(solution)/shard_map/ppermute | solution.py:34
  211.6 82.1 %copy-start.1 = (f32[1,128,3,128]{3,1,2,0:T(8,128)S(1)}, f32[1,128,3,128]{3,1,2,0:T(8,128)}, u32[]{:S(2)}) copy-start(f32[1,128,3,128]{3,1,2,0:T(8,128)} %param.25) | copy-start | bytes 589828
Sparse Core Ops, SparseCore 0:
  10.7 47.9 all-gather.1
  211.7 80.1 reduce-scatter.1
where the time goes:
time: 302 us; the launch traced here: 301 us
  other arithmetic  133 us (44%)
  waiting for transfers between devices  85.7 us (28%)
  local copies, waits for them, and re-layouts  40.2 us (13%)
  between operations  14.3 us (5%)
  starting transfers between devices  13.4 us (4%)
  matrix products  11.9 us (4%)
    reduce_scatter x1, waiting for transfers between devices, local(): lax.psum_scatter(jnp.dot(onehot, deposits, precision=lax.Precision.HIGHES...  79 us
    reduce_sum x24, other arithmetic, pair_forces(): distance = jnp.sqrt(jnp.sum(offset * offset, axis=1) + EPS_DIST)  49.3 us
    reduce_sum x24, other arithmetic, pair_forces(): return jnp.sum(factor[:, None] * offset, axis=3)  44.7 us
    gather x48, local copies, waits for them, and re-layouts, accumulate(): forces = pair_forces(padded[left + G], padded[right])  27.1 us
    div x24, other arithmetic, pair_forces(): factor = intersection * (STIFFNESS - DAMPING * normal_speed) / distance  15.9 us
    lt x24, other arithmetic, accumulate(): is_live = first_row + jnp.arange(PAIR_BATCH, dtype=jnp.int32) < pair_total  15.7 us
    ppermute x3, starting transfers between devices, from_partner(): return lax.ppermute(value, axis, pairs)  7.4 us
  transfers between devices with their start and end apart: 9, of which 5 were waited for; matrix products, arithmetic and copies ran while one was open for 31% of the time, Pallas kernels for 0%

commit v1 on v0

--- a/solution.py
+++ b/solution.py
@@ -1,6 +1,9 @@
 import jax
 import jax.numpy as jnp
 from jax import lax
+from jax.experimental import pallas as pl
+from jax.experimental.pallas import tpu as pltpu
+
 from jax.sharding import PartitionSpec as P
 
 G = 4
@@ -36,33 +39,116 @@
     return block
 
 
-def pair_forces(left_blk, right_blk):
-    offset = left_blk[:, 0:3, :, None] - right_blk[:, 0:3, None, :]
-    distance = jnp.sqrt(jnp.sum(offset * offset, axis=1) + EPS_DIST)
-    intersection = jnp.maximum(left_blk[:, 6, :, None] + right_blk[:, 6, None, :] - distance, 0.0)
-    rel_vel = left_blk[:, 3:6, :, None] - right_blk[:, 3:6, None, :]
-    normal_speed = jnp.sum(rel_vel * offset, axis=1) / distance
-    factor = intersection * (STIFFNESS - DAMPING * normal_speed) / distance
-    return jnp.sum(factor[:, None] * offset, axis=3)
-
-
-def contact_forces(padded, left_ids, right_ids, pair_total, batches):
-    blocks = padded.shape[0] - 2 * G
-    empty_sum = jnp.zeros((blocks, 3 * padded.shape[2]), jnp.float32)
-
-    def accumulate(batch_idx, summed):
-        first_row = batch_idx * PAIR_BATCH
-        left = lax.dynamic_slice_in_dim(left_ids, first_row, PAIR_BATCH)
-        right = lax.dynamic_slice_in_dim(right_ids, first_row, PAIR_BATCH)
-        is_live = first_row + jnp.arange(PAIR_BATCH, dtype=jnp.int32) < pair_total
-        forces = pair_forces(padded[left + G], padded[right])
-        forces = jnp.where(is_live[:, None, None], forces, 0.0)
-        onehot = (jnp.arange(blocks, dtype=jnp.int32)[:, None] == left[None, :]).astype(jnp.float32)
-        return summed + jnp.dot(
-            onehot, forces.reshape(PAIR_BATCH, -1), precision=lax.Precision.HIGHEST
-        )
-
-    return lax.fori_loop(0, batches, accumulate, empty_sum)
+PAIRS = 192
+
+def rowsel(rows, zero):
+    row = lax.broadcasted_iota(jnp.int32, (8, 128), 0)
+    out = zero
+    for k, r in enumerate(rows):
+        if r is not None:
+            out = jnp.where(row == k, r, out)
+    return out
+
+def bf(x):
+    return x.astype(jnp.bfloat16).astype(jnp.float32)
+
+def split3(x):
+    s1 = bf(x)
+    r = x - s1
+    s2 = bf(r)
+    return s1, s2, bf(r - s2)
+
+def centered(blk):
+    row = lax.broadcasted_iota(jnp.int32, (8, 128), 0)
+    return jnp.where(row < 3, blk - 0.5, blk)
+
+def partner_features(blk):
+    row = lax.broadcasted_iota(jnp.int32, (8, 128), 0)
+    y = centered(blk)
+    sq = jnp.sum(y[0:3] * y[0:3], axis=0, keepdims=True)
+    sv = jnp.sum(y[0:3] * y[3:6], axis=0, keepdims=True)
+    s1, s2, s3 = split3(jnp.where(row < 6, y, 1.0))
+    n = split3(sq)
+    s = split3(sv)
+    e = rowsel([n[0], n[1], n[2], s[0], s[1], s[2]], jnp.zeros((8, 128), jnp.float32))
+    return jnp.concatenate([y, s1, s1, s1, s2, s2, s3, e], axis=0)
+
+def local_features(blk):
+    row = lax.broadcasted_iota(jnp.int32, (8, 128), 0)
+    zero = jnp.zeros((8, 128), jnp.float32)
+    y = centered(blk)
+    sq = jnp.sum(y[0:3] * y[0:3], axis=0, keepdims=True) + EPS_DIST
+    sv = jnp.sum(y[0:3] * y[3:6], axis=0, keepdims=True)
+    wd = jnp.where(row < 3, -2.0 * y, jnp.where(row == 6, sq, 0.0))
+    wv = jnp.concatenate([-y[3:6], -y[0:3], sv, jnp.zeros((1, 128), jnp.float32)], axis=0)
+    p1, p2, p3 = split3(wd)
+    v1, v2, v3 = split3(wv)
+    ed = jnp.where(row < 3, 1.0, 0.0)
+    ev = jnp.where((row >= 3) & (row < 6), 1.0, 0.0)
+    d = jnp.concatenate([zero, p1, p2, p3, p1, p2, p1, ed], axis=0)
+    v = jnp.concatenate([zero, v1, v2, v3, v1, v2, v1, ev], axis=0)
+    return jnp.concatenate([d, v], axis=1).astype(jnp.bfloat16)
+
+def prep_partner(blk, j, a_ref, xb_ref):
+    t = partner_features(blk).T
+    a_ref[j] = t.astype(jnp.bfloat16)
+    for k, ch in enumerate((0, 1, 2, 6)):
+        xb_ref[j, k] = jnp.broadcast_to(t[:, ch:ch + 1], (128, 128))
+
+def pair_sums(a, b, a_ref, xb_ref, b_ref, rad_row):
+    z = jnp.dot(a_ref[b], b_ref[a], preferred_element_type=jnp.float32)
+    inv = lax.rsqrt(jnp.maximum(z[:, :128], EPS_DIST))
+    rs = xb_ref[b, 3] + rad_row
+    w = jnp.maximum(rs * inv - 1.0, 0.0)
+    f = w * (STIFFNESS - DAMPING * z[:, 128:] * inv)
+    rows = []
+    for k in range(3):
+        rows.append(jnp.sum(f * xb_ref[b, k], axis=0, keepdims=True))
+    rows.append(jnp.sum(f, axis=0, keepdims=True))
+    return rows
+
+def contact_kernel(ext_ref, ids_ref, left_ref, cnt_ref, out_ref, a_ref, xb_ref, b_ref, f_ref):
+    def prep(j, _):
+        prep_partner(ext_ref[j], j, a_ref, xb_ref)
+        return 0
+    lax.fori_loop(0, 40, prep, 0, unroll=4)
+    def prepl(j, _):
+        b_ref[j] = local_features(ext_ref[j + 4])
+        return 0
+    lax.fori_loop(0, 32, prepl, 0, unroll=4)
+    zero = jnp.zeros((8, 128), jnp.float32)
+    def body(i, _):
+        a = ids_ref[0, i]
+        b = ids_ref[1, i]
+        blk = centered(ext_ref[a + 4])
+        rows = pair_sums(a, b, a_ref, xb_ref, b_ref, blk[6:7])
+        f_ref[i] = rowsel([blk[k:k + 1] * rows[3] - rows[k] for k in range(3)], zero)
+        return 0
+    lax.fori_loop(0, PAIRS, body, 0, unroll=UNROLL)
+    lane = lax.broadcasted_iota(jnp.int32, (32, PAIRS), 1)
+    blkid = lax.broadcasted_iota(jnp.int32, (32, PAIRS), 0)
+    oh = jnp.where((left_ref[0:1] == blkid) & (lane < cnt_ref[0, 0]), 1.0, 0.0).astype(jnp.bfloat16)
+    for k in range(3):
+        s1, s2, s3 = split3(f_ref[:, k, :])
+        acc = jnp.zeros((32, 128), jnp.float32)
+        for s in (s3, s2, s1):
+            acc = acc + jnp.dot(oh, s.astype(jnp.bfloat16), preferred_element_type=jnp.float32)
+        out_ref[k] = acc
+
+UNROLL = 8
+
+def contact_forces(ext, pairs, count):
+    ids = pairs
+    return pl.pallas_call(
+        contact_kernel,
+        out_shape=jax.ShapeDtypeStruct((3, 32, 128), jnp.float32),
+        in_specs=[pl.BlockSpec(memory_space=pltpu.VMEM), pl.BlockSpec(memory_space=pltpu.SMEM),
+                  pl.BlockSpec(memory_space=pltpu.VMEM), pl.BlockSpec(memory_space=pltpu.SMEM)],
+        out_specs=pl.BlockSpec(memory_space=pltpu.VMEM),
+        scratch_shapes=[pltpu.VMEM((40, 128, 64), jnp.bfloat16), pltpu.VMEM((40, 4, 128, 128), jnp.float32),
+                        pltpu.VMEM((32, 64, 256), jnp.bfloat16), pltpu.VMEM((PAIRS, 8, 128), jnp.float32)],
+        compiler_params=pltpu.CompilerParams(vmem_limit_bytes=48 * 1024 * 1024),
+    )(ext, ids, pairs, count)
 
 
 def local(
@@ -104,15 +190,9 @@
     carried = jnp.dot(onehot, shard_piece, preferred_element_type=jnp.float32)
     fluid_blk = carried.astype(jnp.bfloat16).reshape(blocks, 3, cells)
     sampled = jnp.einsum("npc,nkc->nkp", weights, fluid_blk, preferred_element_type=jnp.float32)
-    left_ids = pair_lists[0, 0]
-    right_ids = pair_lists[0, 1]
-    pair_total = pair_counts[0, 0]
     for substep in range(SUBSTEPS):
         padded = with_halo(particle_state, (("dom", 0),), G)
-        contact = contact_forces(
-            padded, left_ids, right_ids, pair_total, left_ids.shape[0] // PAIR_BATCH
-        )
-        contact = contact.reshape(blocks, 3, blk_width)
+        contact = jnp.transpose(contact_forces(padded, pair_lists[0], pair_counts), (1, 0, 2))
         masses = (particle_state[:, 6] / RADIUS_REF) ** 3
         beta = particle_state[:, 7]
         velocity = particle_state[:, 3:6]

time: 302 us -> 176 us (0.58)
  other arithmetic: 133 us -> 5.35 us
  Pallas kernels: 0 us -> 37 us
  local copies, waits for them, and re-layouts: 40.2 us -> 11.2 us
  matrix products: 11.9 us -> 6.76 us
    reduce_sum x48 -> x0, other arithmetic: 94 us -> none  [the longest x24 49.3 us: pair_forces(): distance = jnp.sqrt(jnp.sum(offset * offset, axis=1) + EPS_DIST)]
    pallas_call x0 -> x2, Pallas kernels: none -> 37 us  [contact_forces(): pl.pallas_call(contact_kernel, out_shape=jax.ShapeDtypeStruct((3, 32, 128...]
    gather x48 -> x0, local copies, waits for them, and re-layouts: 27.1 us -> none  [accumulate(): forces = pair_forces(padded[left + G], padded[right])]
    div x24 -> x0, other arithmetic: 15.9 us -> none  [pair_forces(): factor = intersection * (STIFFNESS - DAMPING * normal_speed) / distance]
    lt x24 -> x0, other arithmetic: 15.7 us -> none  [accumulate(): is_live = first_row + jnp.arange(PAIR_BATCH, dtype=jnp.int32) < pair_total]
    dot_general x24 -> x0, matrix products: 5.15 us -> none  [accumulate(): jnp.dot(onehot, forces.reshape(PAIR_BATCH, -1), precision=lax.Precision.H...]
    all_gather x1, waiting for transfers between devices: 0.02 us -> 3.98 us  [local(): shard_piece = lax.all_gather(fluid_bf, 'bis', axis=0, tiled=True)]
    reduce_scatter x1, waiting for transfers between devices: 79 us -> 75.9 us  [local(): lax.psum_scatter(jnp.dot(onehot, deposits, precision=lax.Precision.HIGHES...]
  transfers between devices with their start and end apart: 9 -> 9, of which waited for: 5 -> 6; matrix products, arithmetic and copies ran while one was open for 31% -> 7% of each run, Pallas kernels for 0% -> 11%
where the time goes in v1:
time: 176 us; the launch traced here: 175 us
  waiting for transfers between devices  86.6 us (49%)
  Pallas kernels  37 us (21%)
  between operations  14.9 us (8%)
  starting transfers between devices  13.4 us (8%)
  local copies, waits for them, and re-layouts  11.2 us (6%)
  matrix products  6.76 us (4%)
  other arithmetic  5.35 us (3%)
    reduce_scatter x1, waiting for transfers between devices, local(): lax.psum_scatter(jnp.dot(onehot, deposits, precision=lax.Precision.HIGHES...  75.9 us
    pallas_call x2, Pallas kernels, contact_forces(): pl.pallas_call(contact_kernel, out_shape=jax.ShapeDtypeStruct((3, 32, 128...  37 us
    ppermute x3, starting transfers between devices, from_partner(): return lax.ppermute(value, axis, pairs)  7.4 us
    ppermute x2, starting transfers between devices, with_halo(): lax.ppermute(lax.slice_in_dim(block, 0, width, axis=dim), axis, backward)  5.89 us
    all_gather x1, waiting for transfers between devices, local(): shard_piece = lax.all_gather(fluid_bf, 'bis', axis=0, tiled=True)  3.98 us
    ppermute x3, waiting for transfers between devices, from_partner(): return lax.ppermute(value, axis, pairs)  3.89 us
    dot_general x1, matrix products, local(): jnp.dot(onehot, deposits, precision=lax.Precision.HIGHEST)  3.75 us
  transfers between devices with their start and end apart: 9, of which 6 were waited for; matrix products, arithmetic and copies ran while one was open for 7% of the time, Pallas kernels for 11%

profile of v1, /device:TPU:0, one launch (start us, length us, event | category | flops | bytes accessed | tf_op | source)
XLA Modules:
  0.0 175.2 jit_solution(11017795928210308926)
XLA Ops:
  7.2 0.0 copy-start
  7.2 0.0 copy-start.1
  7.2 0.0 all-gather.2.cloned.1.call-start
  7.2 1.7 copy.26
  9.0 0.0 copy-start.3
  9.0 0.0 all-gather.2.cloned.1.call-update
  9.0 0.0 reduce-scatter.2.cloned.1.call-start
  9.1 0.7 fusion.21
  9.8 0.9 copy_bitcast_fusion
  10.7 0.8 pad_maximum_fusion.2
  11.5 0.6 gather_fusion
  12.0 2.1 %collective-permute-start = (f32[16,8,128]{2,1,0:T(8,128)S(1)}, f32[16,8,128]{2,1,0:T(8,128)S(1)}, u32[]{:S(2)}, u32[]{:S(2)}) collective-permute-start(f32[16,8,128]{2,1,0:T(8,128)S(1)} %gather_fusion), channel_id=1, source_target_pairs={{0,8},{8,0},{16,24},{24,16},{32,40},{40,32},{48,56},{56,48},{64,72... | collective-permute-start | bytes 196616 | tf_op jit(solution)/shard_map/ppermute | solution.py:25
  14.8 1.4 fusion.26
  16.2 0.6 iota_compare_fusion.6
  16.8 0.0 collective-permute-done
  16.8 0.1 broadcast_select_fusion.2
  16.9 1.0 scatter_fusion
  17.9 0.6 gather_fusion.1
  18.5 3.7 %collective-permute-start.1 = (f32[16,8,128]{2,1,0:T(8,128)S(1)}, f32[16,8,128]{2,1,0:T(8,128)S(1)}, u32[]{:S(2)}, u32[]{:S(2)}) collective-permute-start(f32[16,8,128]{2,1,0:T(8,128)S(1)} %gather_fusion.1), channel_id=1, source_target_pairs={{0,16},{8,24},{16,0},{24,8},{32,48},{40,56},{48,32},{56,40},{64,80... | collective-permute-start | bytes 196616 | tf_op jit(solution)/shard_map/ppermute | solution.py:25
  22.2 0.7 iota_compare_fusion.5
  22.8 1.6 collective-permute-done.1
  24.4 0.1 broadcast_select_fusion.1
  24.5 1.0 scatter_fusion.1
  25.5 0.6 gather_fusion.2
  26.1 1.7 collective-permute-start.2
  27.8 0.6 iota_compare_fusion.4
  28.4 2.3 %collective-permute-done.2 = f32[16,8,128]{2,1,0:T(8,128)S(1)} collective-permute-done((f32[16,8,128]{2,1,0:T(8,128)S(1)}, f32[16,8,128]{2,1,0:T(8,128)S(1)}, u32[]{:S(2)}, u32[]{:S(2)}) %collective-permute-start.2) | collective-permute-done | bytes 65568 | tf_op jit(solution)/shard_map/ppermute | solution.py:25
  30.7 0.1 broadcast_select_fusion
  30.8 1.0 scatter_fusion.2
  31.9 0.0 collective-permute-start.3
  31.9 2.9 %collective-permute-start.4 = (f32[4,8,128]{2,1,0:T(8,128)S(1)}, f32[4,8,128]{2,1,0:T(8,128)S(1)}, u32[]{:S(2)}, u32[]{:S(2)}) collective-permute-start(f32[4,8,128]{2,1,0:T(8,128)S(1)} %get-tuple-element.21), channel_id=1, source_target_pairs={{1,0},{2,1},{3,2},{4,3},{5,4},{6,5},{7,6},{0,7},{9,8},{10,9},{11,1... | collective-permute-start | bytes 49160 | tf_op jit(solution)/shard_map/ppermute | solution.py:37
  34.9 1.3 collective-permute-done.3
  36.2 0.0 collective-permute-done.4
  36.3 0.0 copy-done.1
  36.3 18.5 %shard_map.138 = f32[3,32,128]{2,1,0:T(8,128)S(1)} custom-call(f32[40,8,128]{2,1,0:T(8,128)S(1)} %pad_maximum_fusion.ext_ref, s32[2,192]{1,0:T(2,128)S(1)} %bitcast.70, s32[2,192]{1,0:T(2,128)S(1)} %bitcast.71, s32[1,1]{1,0:T(1,128)S(6)} %copy.59.cnt_ref), custom_call_target="tpu_custom_call" | custom-call | tf_op jit(solution)/shard_map/pallas_call | solution.py:142
  54.8 4.0 %all-gather.2.cloned.1.call-done = bf16[2048,384]{0,1:T(8,128)(2,1)} async-done(((bf16[128,384]{0,1:T(8,128)(2,1)}), bf16[2048,384]{0,1:T(8,128)(2,1)}) %all-gather.2.cloned.1.call-update) | async-done | bytes 1572880 | tf_op jit(solution)/shard_map/all_gather | solution.py:186
  58.8 0.0 copy-done.3
  58.8 2.0 %convolution_convert_fusion = bf16[32,384]{1,0:T(8,128)(2,1)S(1)} fusion(bf16[2048,384]{0,1:T(8,128)(2,1)} %all-gather.2.cloned.1.call-done, s32[32]{0:T(128)S(1)} %bitcast.86), kind=kOutput, calls=%fused_computation.6 | convolution fusion | flops 50409472 | bytes 1597568 | tf_op jit(solution)/shard_map/dot_general | solution.py:190
  60.8 0.0 copy-done
  60.8 0.7 slice_add_fusion
  61.5 0.0 collective-permute-start.5
  61.5 2.9 %collective-permute-start.6 = (f32[4,8,128]{2,1,0:T(8,128)S(1)}, f32[4,8,128]{2,1,0:T(8,128)S(1)}, u32[]{:S(2)}, u32[]{:S(2)}) collective-permute-start(f32[4,8,128]{2,1,0:T(8,128)S(1)} %get-tuple-element.19), channel_id=1, source_target_pairs={{1,0},{2,1},{3,2},{4,3},{5,4},{6,5},{7,6},{0,7},{9,8},{10,9},{11,1... | collective-permute-start | bytes 49160 | tf_op jit(solution)/shard_map/ppermute | solution.py:37
  64.4 1.4 collective-permute-done.5
  65.8 0.0 collective-permute-done.6
  65.9 18.5 %shard_map.139 = f32[3,32,128]{2,1,0:T(8,128)S(1)} custom-call(f32[40,8,128]{2,1,0:T(8,128)S(1)} %pad_maximum_fusion.1.ext_ref, s32[2,192]{1,0:T(2,128)S(1)} %bitcast.72, s32[2,192]{1,0:T(2,128)S(1)} %bitcast.73, s32[1,1]{1,0:T(1,128)S(6)} %copy.59.cnt_ref), custom_call_target="tpu_custom_call" | custom-call | tf_op jit(solution)/shard_map/pallas_call | solution.py:142
  84.4 0.1 multiply_convert_fusion
  84.5 0.4 fusion
  84.9 3.7 %fusion.4 = f32[2048,512]{1,0:T(8,128)} fusion(s32[32]{0:T(128)S(1)} %bitcast.87, f32[4,8,4,128]{3,2,1,0:T(4,128)S(1)} %bitcast.77), kind=kOutput, calls=%fused_computation.12 | convolution fusion | flops 402718720 | bytes 4259968 | tf_op jit(solution)/shard_map/dot_general | solution.py:216
  88.7 0.0 copy-start.2
  88.7 0.0 reduce-scatter.2.cloned.1.call-update
  88.7 0.6 copy.30
  89.3 0.6 copy.31
  90.0 75.9 %reduce-scatter.2.cloned.1.call-done = f32[128,512]{1,0:T(8,128)} async-done(((f32[2048,512]{1,0:T(8,128)}), f32[128,512]{1,0:T(8,128)}) %reduce-scatter.2.cloned.1.call-update) | async-done | bytes 262160 | tf_op jit(solution)/shard_map/reduce_scatter | solution.py:215
  165.9 1.0 reshape.136
  166.9 0.1 slice.88
  167.0 0.6 divide_bitcast_fusion
  167.6 0.0 copy-done.2
  167.6 0.7 fusion.8
  (12 shorter events, 0.2 us)
Async XLA Ops:
  7.2 53.6 %copy-start = (bf16[1,32,128,128]{3,2,1,0:T(8,128)(2,1)S(1)}, bf16[1,32,128,128]{3,2,1,0:T(8,128)(2,1)}, u32[]{:S(2)}) copy-start(bf16[1,32,128,128]{3,2,1,0:T(8,128)(2,1)} %param.20) | copy-start | bytes 3145732
  7.2 29.1 %copy-start.1 = (s32[1,2,192]{2,1,0:T(2,128)S(1)}, s32[1,2,192]{2,1,0:T(2,128)}, u32[]{:S(2)}) copy-start(s32[1,2,192]{2,1,0:T(2,128)} %param.17) | copy-start | bytes 4612
  7.2 51.6 %all-gather.2.cloned.1.call-start = ((), (), s32[]{:S(2)}) async-start(), calls=%async_computation.1 | async-start | bytes 1671168 | tf_op jit(solution)/shard_map/all_gather | solution.py:186
  9.0 49.8 %copy-start.3 = (s32[1,32]{1,0:T(1,128)S(1)}, s32[1,32]{1,0:T(1,128)}, u32[]{:S(2)}) copy-start(s32[1,32]{1,0:T(1,128)} %param.19) | copy-start | bytes 388
  9.0 156.9 %reduce-scatter.2.cloned.1.call-start = ((), (), s32[]{:S(2)}) async-start(), calls=%async_computation.2 | async-start | bytes 4456448 | tf_op jit(solution)/shard_map/reduce_scatter | solution.py:215
  12.0 4.8 %collective-permute-start = (f32[16,8,128]{2,1,0:T(8,128)S(1)}, f32[16,8,128]{2,1,0:T(8,128)S(1)}, u32[]{:S(2)}, u32[]{:S(2)}) collective-permute-start(f32[16,8,128]{2,1,0:T(8,128)S(1)} %gather_fusion), channel_id=1, source_target_pairs={{0,8},{8,0},{16,24},{24,16},{32,40},{40,32},{48,56},{56,48},{64,72... | collective-permute-start | bytes 196616 | tf_op jit(solution)/shard_map/ppermute | solution.py:25
  18.5 5.9 %collective-permute-start.1 = (f32[16,8,128]{2,1,0:T(8,128)S(1)}, f32[16,8,128]{2,1,0:T(8,128)S(1)}, u32[]{:S(2)}, u32[]{:S(2)}) collective-permute-start(f32[16,8,128]{2,1,0:T(8,128)S(1)} %gather_fusion.1), channel_id=1, source_target_pairs={{0,16},{8,24},{16,0},{24,8},{32,48},{40,56},{48,32},{56,40},{64,80... | collective-permute-start | bytes 196616 | tf_op jit(solution)/shard_map/ppermute | solution.py:25
  26.1 4.6 %collective-permute-start.2 = (f32[16,8,128]{2,1,0:T(8,128)S(1)}, f32[16,8,128]{2,1,0:T(8,128)S(1)}, u32[]{:S(2)}, u32[]{:S(2)}) collective-permute-start(f32[16,8,128]{2,1,0:T(8,128)S(1)} %gather_fusion.2), channel_id=1, source_target_pairs={{0,32},{8,40},{16,48},{24,56},{32,0},{40,8},{48,16},{56,24},{64,96... | collective-permute-start | bytes 196616 | tf_op jit(solution)/shard_map/ppermute | solution.py:25
  31.9 4.4 %collective-permute-start.3 = (f32[4,8,128]{2,1,0:T(8,128)S(1)}, f32[4,8,128]{2,1,0:T(8,128)S(1)}, u32[]{:S(2)}, u32[]{:S(2)}) collective-permute-start(f32[4,8,128]{2,1,0:T(8,128)S(1)} %get-tuple-element.20), channel_id=1, source_target_pairs={{0,1},{1,2},{2,3},{3,4},{4,5},{5,6},{6,7},{7,0},{8,9},{9,10},{10,1... | collective-permute-start | bytes 49160 | tf_op jit(solution)/shard_map/ppermute | solution.py:34
  31.9 4.4 %collective-permute-start.4 = (f32[4,8,128]{2,1,0:T(8,128)S(1)}, f32[4,8,128]{2,1,0:T(8,128)S(1)}, u32[]{:S(2)}, u32[]{:S(2)}) collective-permute-start(f32[4,8,128]{2,1,0:T(8,128)S(1)} %get-tuple-element.21), channel_id=1, source_target_pairs={{1,0},{2,1},{3,2},{4,3},{5,4},{6,5},{7,6},{0,7},{9,8},{10,9},{11,1... | collective-permute-start | bytes 49160 | tf_op jit(solution)/shard_map/ppermute | solution.py:37
  61.5 4.4 %collective-permute-start.5 = (f32[4,8,128]{2,1,0:T(8,128)S(1)}, f32[4,8,128]{2,1,0:T(8,128)S(1)}, u32[]{:S(2)}, u32[]{:S(2)}) collective-permute-start(f32[4,8,128]{2,1,0:T(8,128)S(1)} %get-tuple-element.18), channel_id=1, source_target_pairs={{0,1},{1,2},{2,3},{3,4},{4,5},{5,6},{6,7},{7,0},{8,9},{9,10},{10,1... | collective-permute-start | bytes 49160 | tf_op jit(solution)/shard_map/ppermute | solution.py:34
  61.5 4.4 %collective-permute-start.6 = (f32[4,8,128]{2,1,0:T(8,128)S(1)}, f32[4,8,128]{2,1,0:T(8,128)S(1)}, u32[]{:S(2)}, u32[]{:S(2)}) collective-permute-start(f32[4,8,128]{2,1,0:T(8,128)S(1)} %get-tuple-element.19), channel_id=1, source_target_pairs={{1,0},{2,1},{3,2},{4,3},{5,4},{6,5},{7,6},{0,7},{9,8},{10,9},{11,1... | collective-permute-start | bytes 49160 | tf_op jit(solution)/shard_map/ppermute | solution.py:37
  88.7 79.0 %copy-start.2 = (f32[1,128,3,128]{3,1,2,0:T(8,128)S(1)}, f32[1,128,3,128]{3,1,2,0:T(8,128)}, u32[]{:S(2)}) copy-start(f32[1,128,3,128]{3,1,2,0:T(8,128)} %param.21) | copy-start | bytes 589828
Sparse Core Ops, SparseCore 0:
  10.7 47.9 all-gather.1
  88.8 77.0 reduce-scatter.1

commit v2 on v0

v2 whole, which is shorter than its diff:
```python
import functools

import jax
import jax.numpy as jnp
from jax import lax
from jax.experimental import pallas as pl
from jax.experimental.pallas import tpu as pltpu
from jax.sharding import PartitionSpec as P

G = 4
SUBSTEPS = 2
BLK = 128

STIFFNESS = 5.0
DAMPING = 1.0
TIME_STEP = 0.05
EPS_DIST = 0.0001
RADIUS_REF = 0.1
FLUID_GAIN = 0.2

F32 = jnp.float32
BF16 = jnp.bfloat16
MESH = pl.DeviceIdType.MESH


def row_ids():
    return lax.broadcasted_iota(jnp.int32, (8, BLK), 0)


def stack_rows(rows):
    row = row_ids()
    out = jnp.zeros((8, BLK), F32)
    for k, value in enumerate(rows):
        out = jnp.where(row == k, value, out)
    return out


def split(x, parts=3):
    out = []
    for _ in range(parts):
        piece = x.astype(BF16).astype(F32)
        out.append(piece)
        x = x - piece
    return out


def centered(blk):
    return jnp.where(row_ids() < 3, blk - 0.5, blk)


def partner_features(blk):
    row = row_ids()
    y = centered(blk)
    sq = jnp.sum(y[0:3] * y[0:3], axis=0, keepdims=True)
    sv = jnp.sum(y[0:3] * y[3:6], axis=0, keepdims=True)
    base = jnp.where(row < 6, y, jnp.where(row == 6, 1.0, y[6:7]))
    s1, s2, s3 = split(base)
    e = stack_rows(split(sq) + split(sv))
    zero = jnp.zeros((8, BLK), F32)
    return jnp.concatenate([zero, s1, s1, s1, s2, s2, s3, e], axis=0)


def local_features(blk):
    row = row_ids()
    zero = jnp.zeros((8, BLK), F32)
    y = centered(blk)
    sq = jnp.sum(y[0:3] * y[0:3], axis=0, keepdims=True) + EPS_DIST
    sv = jnp.sum(y[0:3] * y[3:6], axis=0, keepdims=True)
    wd = jnp.where(row < 3, -2.0 * y, jnp.where(row == 6, sq, 0.0))
    wv = jnp.concatenate([-y[3:6], -y[0:3], sv, jnp.zeros((1, BLK), F32)], axis=0)
    p1, p2, p3 = split(wd)
    v1, v2, v3 = split(wv)
    ed = jnp.where(row < 3, 1.0, 0.0)
    ev = jnp.where((row >= 3) & (row < 6), 1.0, 0.0)
    d = jnp.concatenate([zero, p1, p2, p3, p1, p2, p1, ed], axis=0)
    v = jnp.concatenate([zero, v1, v2, v3, v1, v2, v1, ev], axis=0)
    return jnp.concatenate([d, v], axis=1).astype(BF16)


def kernel(
    bis, dom, pmax,
    pos_ref, vel_ref, rad_ref, drag_ref, slots_ref, inv_ref, pairs_ref, left_ref, cnt_ref, own_ref, w_hbm, fluid_ref,
    pos_out, vel_out, fluid_out, void_out,
    st0, st1, mig_s, mig_r, halo_r, own_s, own_r, fl_s, fl_r, w_v, flrow, samp,
    a_ref, xb_ref, b_ref, f_ref, sel_ref, oh_ref, dep, dep_s, dep_r,
    w_sem, mig_ss, mig_rs, halo_ss, halo_rs, own_ss, own_rs, fl_ss, fl_rs, dep_ss, dep_rs,
):
    nb = st0.shape[0]
    per = BLK // nb
    tiles = bis // per
    me = lax.axis_index("bis")
    mine = lax.axis_index("dom")
    right, left = lax.rem(mine + 1, dom), lax.rem(mine + dom - 1, dom)

    weights_copy = pltpu.make_async_copy(w_hbm, w_v, w_sem)
    weights_copy.start()

    barrier = pltpu.get_barrier_semaphore()

    def greet(r, _):
        pl.semaphore_signal(barrier, inc=1, device_id={"bis": lax.rem(me + r, bis)}, device_id_type=MESH)
        return 0

    lax.fori_loop(1, bis, greet, 0)
    for side in (left, right):
        pl.semaphore_signal(barrier, inc=1, device_id={"dom": side}, device_id_type=MESH)

    def to_peer(r, source, target, ss, rs):
        peer = lax.rem(me + r, bis)
        return pltpu.make_async_remote_copy(
            src_ref=source(peer), dst_ref=target.at[me], send_sem=ss.at[r], recv_sem=rs.at[r],
            device_id={"bis": peer}, device_id_type=MESH,
        )

    def start_all(source, target, ss, rs):
        def step(r, _):
            to_peer(r, source, target, ss, rs).start()
            return 0

        lax.fori_loop(1, bis, step, 0)

    def wait_all(source, target, ss, rs):
        def step(r, _):
            to_peer(r, source, target, ss, rs).wait()
            return 0

        lax.fori_loop(1, bis, step, 0)

    for k in range(3):
        st0[:, k, :] = pos_ref[k]
        st0[:, 3 + k, :] = vel_ref[k]
    st0[:, 6, :] = rad_ref[...]
    st0[:, 7, :] = drag_ref[...]
    lane8 = lax.broadcasted_iota(jnp.int32, (8, BLK), 1)
    quarter = lax.rem(me, per)
    own_s[...] = jnp.where(lane8 // nb == quarter, own_ref[...], 0)
    own_r[me] = own_s[...]

    capacity = mig_s.shape[1]

    def gather(level):
        def step(j, _):
            mig_s[level, j] = st0[slots_ref[level, j]]
            return 0

        lax.fori_loop(0, capacity, step, 0, unroll=4)

    def migrate_copy(level):
        stride = 2**level
        bit = lax.rem(me // stride, 2)
        partner = me + stride - 2 * stride * bit
        return pltpu.make_async_remote_copy(
            src_ref=mig_s.at[level], dst_ref=mig_r[level], send_sem=mig_ss.at[level], recv_sem=mig_rs.at[level],
            device_id={"bis": partner}, device_id_type=MESH,
        )

    def scatter(level):
        def step(n, _):
            j = inv_ref[level, n]
            st0[n] = jnp.where(j >= 0, mig_r[level][jnp.maximum(j, 0)], st0[n])
            return 0

        lax.fori_loop(0, nb, step, 0, unroll=4)

    gather(0)
    pl.semaphore_wait(barrier, bis - 1 + 2)
    migrate_copy(0).start()
    own_source = lambda peer: own_s
    start_all(own_source, own_r, own_ss, own_rs)
    srow = lax.broadcasted_iota(jnp.int32, (64, BLK), 0)
    part = (srow >= 8) & (srow < 56)
    first = (srow // 8 == 1) | (srow // 8 == 4) | (srow // 8 == 6)
    for c, ch in enumerate((0, 1, 2, 7)):
        sel_ref[:, c * BLK:(c + 1) * BLK] = jnp.where(first & part & (lax.rem(srow, 8) == ch), 1.0, 0.0).astype(BF16)
    migrate_copy(0).wait()
    scatter(0)
    gather(1)
    migrate_copy(1).start()

    wait_all(own_source, own_r, own_ss, own_rs)
    fluid_bf = jnp.concatenate([fluid_ref[k].astype(BF16) for k in range(3)], axis=1)
    rows = []
    for t in range(tiles):
        row = own_r[per * t, 0:1, :]
        for i in range(1, per):
            row = row + own_r[per * t + i, 0:1, :]
        rows.append(row - BLK * me)
    sub = lax.broadcasted_iota(jnp.int32, (BLK, BLK), 0)
    for t in range(tiles):
        hot = jnp.where(sub == rows[t], 1.0, 0.0)
        oh_ref[t] = hot.astype(BF16)
        chosen = jnp.dot(hot.T.astype(BF16), fluid_bf, preferred_element_type=F32).astype(BF16)
        for i in range(per):
            fl_s[per * t + i] = chosen[nb * i:nb * (i + 1)]
    fl_r[me] = fl_s[me]

    migrate_copy(1).wait()
    scatter(1)
    gather(2)
    migrate_copy(2).start()
    migrate_copy(2).wait()
    scatter(2)

    def halo_copies(step, state):
        return [
            pltpu.make_async_remote_copy(
                src_ref=state.at[pl.ds(nb - G, G)], dst_ref=halo_r.at[step, pl.ds(0, G)],
                send_sem=halo_ss.at[step, 0], recv_sem=halo_rs.at[step, 0],
                device_id={"dom": right}, device_id_type=MESH,
            ),
            pltpu.make_async_remote_copy(
                src_ref=state.at[pl.ds(0, G)], dst_ref=halo_r.at[step, pl.ds(G, G)],
                send_sem=halo_ss.at[step, 1], recv_sem=halo_rs.at[step, 1],
                device_id={"dom": left}, device_id_type=MESH,
            ),
        ]

    fl_source = lambda peer: fl_s.at[peer]

    def prepare(blk, j):
        t = partner_features(blk).T.astype(BF16)
        a_ref[j] = t
        wide = jnp.dot(t, sel_ref[...], preferred_element_type=F32)
        for c in range(4):
            xb_ref[j, c] = wide[:, c * BLK:(c + 1) * BLK]

    def contacts(step, state):
        for copy in halo_copies(step, state):
            copy.start()
        if step == 0:
            start_all(fl_source, fl_r, fl_ss, fl_rs)

        def own_blocks(n, _):
            blk = state[n]
            prepare(blk, n + G)
            b_ref[n] = local_features(blk)
            return 0

        lax.fori_loop(0, nb, own_blocks, 0, unroll=4)
        for copy in halo_copies(step, state):
            copy.wait()

        def rim(n, _):
            prepare(halo_r[step, n], n)
            prepare(halo_r[step, n + G], n + nb + G)
            return 0

        lax.fori_loop(0, G, rim, 0, unroll=2)

        def pair(i, _):
            a = jnp.minimum(pairs_ref[0, i], nb - 1)
            b = pairs_ref[1, i]
            blk = centered(state[a])
            z = jnp.dot(a_ref[b], b_ref[a], preferred_element_type=F32)
            inv = lax.rsqrt(jnp.maximum(z[:, :BLK], EPS_DIST))
            depth = jnp.maximum((xb_ref[b, 3] + blk[6:7]) * inv - 1.0, 0.0)
            f = depth * (STIFFNESS - DAMPING * z[:, BLK:] * inv)
            total = jnp.sum(f, axis=0, keepdims=True)
            f_ref[i] = stack_rows([
                blk[k:k + 1] * total - jnp.sum(f * xb_ref[b, k], axis=0, keepdims=True) for k in range(3)
            ])
            return 0

        lax.fori_loop(0, pmax, pair, 0, unroll=min(16, pmax))
        lane = lax.broadcasted_iota(jnp.int32, (nb, pmax), 1)
        blk_id = lax.broadcasted_iota(jnp.int32, (nb, pmax), 0)
        hot = jnp.where((left_ref[...] == blk_id) & (lane < cnt_ref[0, 0]), 1.0, 0.0).astype(BF16)
        out = []
        for k in range(3):
            acc = jnp.zeros((nb, BLK), F32)
            for piece in split(f_ref[:, k, :])[::-1]:
                acc = acc + jnp.dot(hot, piece.astype(BF16), preferred_element_type=F32)
            out.append(acc)
        return out

    def sample():
        wait_all(fl_source, fl_r, fl_ss, fl_rs)
        total = fl_r[0].astype(F32)
        for g in range(1, bis):
            total = total + fl_r[g].astype(F32)
        flrow[...] = jnp.zeros(flrow.shape, F32)
        for k in range(3):
            flrow[:, k, :] = total[:, k * BLK:(k + 1) * BLK]
        weights_copy.wait()

        def step(n, _):
            samp[n] = lax.dot_general(
                flrow[n].astype(BF16), w_v[n], (((1,), (1,)), ((), ())), preferred_element_type=F32
            )
            return 0

        lax.fori_loop(0, nb, step, 0, unroll=8)

    radius, beta = None, None
    for substep in range(SUBSTEPS):
        state = (st0, st1)[substep]
        contact = contacts(substep, state)
        if substep == 0:
            sample()
            sampled = [samp[:, k, :] for k in range(3)]
            radius, beta = st0[:, 6, :], st0[:, 7, :]
            masses = (radius / RADIUS_REF) ** 3
        speed, place = [], []
        for k in range(3):
            v = state[:, 3 + k, :]
            v = v + TIME_STEP * (contact[k] / masses + beta * (sampled[k] - v))
            speed.append(v)
            place.append(state[:, k, :] + TIME_STEP * v)
        if substep + 1 < SUBSTEPS:
            for k in range(3):
                st1[:, k, :] = place[k]
                st1[:, 3 + k, :] = speed[k]
            st1[:, 6, :] = radius
            st1[:, 7, :] = beta
    for k in range(3):
        pos_out[k] = place[k]
        vel_out[k] = speed[k]

    flrow[...] = jnp.zeros(flrow.shape, F32)
    for k in range(3):
        flrow[:, k, :] = (masses * beta) * (sampled[k] - speed[k])
    flrow[:, 3, :] = masses

    def deposit(n, _):
        dep[n] = jnp.dot(flrow[n].astype(BF16), w_v[n], preferred_element_type=F32)
        return 0

    lax.fori_loop(0, nb, deposit, 0, unroll=8)
    for k in range(4):
        dep_s[k] = dep[:, k, :]
    dep_source = lambda peer: dep_s
    start_all(dep_source, dep_r, dep_ss, dep_rs)
    dep_r[me] = dep_s[...]
    wait_all(dep_source, dep_r, dep_ss, dep_rs)
    totals = []
    for k in (3, 0, 1, 2):
        acc = jnp.zeros((BLK, BLK), F32)
        for t in range(tiles):
            values = dep_r[per * t:per * (t + 1), k].reshape(BLK, BLK)
            for piece in split(values)[::-1]:
                acc = acc + jnp.dot(oh_ref[t], piece.astype(BF16), preferred_element_type=F32)
        totals.append(acc)
    void = 1.0 / (1.0 + totals[0])
    void_out[...] = void
    for k in range(3):
        fluid_out[k] = fluid_ref[k] - FLUID_GAIN * totals[1 + k] * void


def local(
    bis, dom, positions, velocities, radii, drag_rates, mig_slots, mig_counts, pair_lists, pair_counts, owners, dep_weights, fluid_velocity,
):
    nb = positions.shape[1]
    levels, capacity = mig_slots.shape[1:]
    pmax = pair_lists.shape[2]
    fb = fluid_velocity.shape[1]
    j = jnp.arange(capacity, dtype=jnp.int32)
    hit = mig_slots[0][:, None, :] == jnp.arange(nb, dtype=jnp.int32)[None, :, None]
    hit = hit & (j[None, None, :] < mig_counts[0][:, None, None])
    inverse = jnp.max(jnp.where(hit, j[None, None, :], -1), axis=2)
    vmem = pl.BlockSpec(memory_space=pltpu.VMEM)
    smem = pl.BlockSpec(memory_space=pltpu.SMEM)
    dma = pltpu.SemaphoreType.DMA
    tiles = bis * nb // BLK
    outs = pl.pallas_call(
        functools.partial(kernel, bis, dom, pmax),
        out_shape=(
            jax.ShapeDtypeStruct((3, nb, BLK), F32),
            jax.ShapeDtypeStruct((3, nb, BLK), F32),
            jax.ShapeDtypeStruct((3, fb, BLK), F32),
            jax.ShapeDtypeStruct((fb, BLK), F32),
        ),
        in_specs=[vmem] * 4 + [smem] * 3 + [vmem, smem, vmem, pl.BlockSpec(memory_space=pl.ANY), vmem],
        out_specs=(vmem,) * 4,
        scratch_shapes=[
            pltpu.VMEM((nb, 8, BLK), F32),
            pltpu.VMEM((nb, 8, BLK), F32),
            pltpu.VMEM((levels, capacity, 8, BLK), F32),
            [pltpu.VMEM((capacity, 8, BLK), F32)] * levels,
            pltpu.VMEM((SUBSTEPS, 2 * G, 8, BLK), F32),
            pltpu.VMEM((8, BLK), jnp.int32),
            pltpu.VMEM((bis, 8, BLK), jnp.int32),
            pltpu.VMEM((bis, nb, 3 * BLK), BF16),
            pltpu.VMEM((bis, nb, 3 * BLK), BF16),
            pltpu.VMEM((nb, BLK, BLK), BF16),
            pltpu.VMEM((nb, 8, BLK), F32),
            pltpu.VMEM((nb, 8, BLK), F32),
            pltpu.VMEM((nb + 2 * G, BLK, 64), BF16),
            pltpu.VMEM((nb + 2 * G, 4, BLK, BLK), F32),
            pltpu.VMEM((nb, 64, 2 * BLK), BF16),
            pltpu.VMEM((pmax, 8, BLK), F32),
            pltpu.VMEM((64, 4 * BLK), BF16),
            pltpu.VMEM((tiles, BLK, BLK), BF16),
            pltpu.VMEM((nb, 8, BLK), F32),
            pltpu.VMEM((4, nb, BLK), F32),
            pltpu.VMEM((bis, 4, nb, BLK), F32),
            dma,
            dma((levels,)),
            dma((levels,)),
            dma((SUBSTEPS, 2)),
            dma((SUBSTEPS, 2)),
            dma((bis,)),
            dma((bis,)),
            dma((bis,)),
            dma((bis,)),
            dma((bis,)),
            dma((bis,)),
        ],
        compiler_params=pltpu.CompilerParams(
            collective_id=0, has_side_effects=True, vmem_limit_bytes=48 * 1024 * 1024
        ),
    )(
        jnp.transpose(positions[0], (1, 0, 2)),
        jnp.transpose(velocities[0], (1, 0, 2)),
        radii[0],
        drag_rates[0],
        mig_slots[0],
        inverse,
        pair_lists[0],
        pair_lists[0, 0:1],
        pair_counts,
        jnp.tile(owners, (1, BLK // nb)),
        dep_weights[0],
        jnp.transpose(fluid_velocity[0], (1, 0, 2)),
    )
    pos, vel, fluid, void = outs
    return (
        jnp.transpose(pos, (1, 0, 2))[None],
        jnp.transpose(vel, (1, 0, 2))[None],
        jnp.transpose(fluid, (1, 0, 2))[None],
        void[None],
    )


def solution(mesh):
    in_specs = (
        P("bis", "dom", None, None),
        P("bis", "dom", None, None),
        P("bis", "dom", None),
        P("bis", "dom", None),
        P("bis", "dom", None),
        P("bis", "dom"),
        P("bis", None, "dom"),
        P("bis", "dom"),
        P("bis", "dom"),
        P("bis", "dom", None, None),
        P("dom", "bis", None, None),
    )
    out_specs = (
        P("bis", "dom", None, None),
        P("bis", "dom", None, None),
        P("dom", "bis", None, None),
        P("dom", "bis", None),
    )
    body = functools.partial(local, mesh.shape["bis"], mesh.shape["dom"])
    return jax.shard_map(body, mesh=mesh, in_specs=in_specs, out_specs=out_specs, check_vma=False)
```

time: 302 us -> 77.8 us (0.26)
  other arithmetic: 133 us -> 0.17 us
  waiting for transfers between devices: 85.7 us -> 0 us
  Pallas kernels: 0 us -> 67.8 us
  local copies, waits for them, and re-layouts: 40.2 us -> 6.98 us
  starting transfers between devices: 13.4 us -> 0 us
  between operations: 14.3 us -> 1.39 us
  matrix products: 11.9 us -> 0 us
    reduce_sum x48 -> x0, other arithmetic: 94 us -> none  [the longest x24 49.3 us: pair_forces(): distance = jnp.sqrt(jnp.sum(offset * offset, axis=1) + EPS_DIST)]
    reduce_scatter x1 -> x0, waiting for transfers between devices: 79 us -> none  [local(): lax.psum_scatter(jnp.dot(onehot, deposits, precision=lax.Precision.HIGHES...]
    pallas_call x0 -> x1, Pallas kernels: none -> 67.8 us  [local(): pl.pallas_call(functools.partial(kernel, bis, dom, pmax), out_shape=(jax....]
    gather x51 -> x0, local copies, waits for them, and re-layouts: 28.8 us -> none  [the longest x48 27.1 us: accumulate(): forces = pair_forces(padded[left + G], padded[right])]
    lt x27 -> x1, other arithmetic: 17.6 us -> 0.07 us  [local(): hit = hit & (j[None, None, :] < mig_counts[0][:, None, None])]
    div x25 -> x0, other arithmetic: 16.6 us -> none  [the longest x24 15.9 us: pair_forces(): factor = intersection * (STIFFNESS - DAMPING * normal_speed) / distance]
    ppermute x7 -> x0, starting transfers between devices: 13.3 us -> none  [the longest x3 7.4 us: from_partner(): return lax.ppermute(value, axis, pairs)]
    dot_general x28 -> x0, matrix products: 11.9 us -> none  [the longest x24 5.15 us: accumulate(): jnp.dot(onehot, forces.reshape(PAIR_BATCH, -1), precision=lax.Precision.H...]
  transfers between devices with their start and end apart: 9 -> 0, of which waited for: 5 -> 0; matrix products, arithmetic and copies ran while one was open for 31% -> 0% of each run, Pallas kernels for 0% -> 0%
where the time goes in v2:
time: 77.8 us; the launch traced here: 76.3 us
  Pallas kernels  67.8 us (87%)
  local copies, waits for them, and re-layouts  6.98 us (9%)
  between operations  1.39 us (2%)
    pallas_call x1, Pallas kernels, local(): pl.pallas_call(functools.partial(kernel, bis, dom, pmax), out_shape=(jax....  67.8 us
    unnamed x25, local copies, waits for them, and re-layouts  6.89 us

profile of v2, /device:TPU:0, one launch (start us, length us, event | category | flops | bytes accessed | tf_op | source)
XLA Modules:
  0.0 76.3 jit_solution(7889457251091998504)
XLA Ops:
  0.6 0.0 copy-start.9
  0.6 0.0 copy-start.8
  1.3 0.0 copy-start.6
  1.3 0.0 copy-start.7
  1.3 0.0 copy-start.4
  1.3 0.0 copy-start.5
  1.4 0.0 copy-done.9
  1.4 0.1 iota_compare_fusion.1
  1.4 0.6 copy-done.6
  2.0 0.0 copy-done.7
  2.0 0.1 select_reduce_fusion.inv_ref
  2.1 0.0 copy-done.8
  2.1 0.1 tile.13.own_ref
  2.2 0.0 copy-done.4
  2.2 0.0 copy-done.5
  2.2 0.0 copy-start
  2.2 1.2 %copy-done = bf16[1,32,128,128]{3,2,1,0:T(8,128)(2,1)S(1)} copy-done((bf16[1,32,128,128]{3,2,1,0:T(8,128)(2,1)S(1)}, bf16[1,32,128,128]{3,2,1,0:T(8,128)(2,1)}, u32[]{:S(2)}) %copy-start) | copy-done | bytes 1048600
  3.5 0.0 copy-start.1
  3.5 0.9 %copy-done.1 = f32[1,128,3,128]{3,1,2,0:T(8,128)S(1)} copy-done((f32[1,128,3,128]{3,1,2,0:T(8,128)S(1)}, f32[1,128,3,128]{3,1,2,0:T(8,128)}, u32[]{:S(2)}) %copy-start.1) | copy-done | bytes 196632
  4.4 0.0 copy-start.2
  4.4 0.8 %copy-done.2 = f32[1,32,3,128]{3,1,2,0:T(8,128)S(1)} copy-done((f32[1,32,3,128]{3,1,2,0:T(8,128)S(1)}, f32[1,32,3,128]{3,1,2,0:T(8,128)}, u32[]{:S(2)}) %copy-start.2) | copy-done | bytes 49176
  5.2 0.0 copy-start.3
  5.2 0.8 %copy-done.3 = f32[1,32,3,128]{3,1,2,0:T(8,128)S(1)} copy-done((f32[1,32,3,128]{3,1,2,0:T(8,128)S(1)}, f32[1,32,3,128]{3,1,2,0:T(8,128)}, u32[]{:S(2)}) %copy-start.3) | copy-done | bytes 49176
  6.0 67.8 %shard_map.138 = (f32[3,32,128]{2,1,0:T(8,128)S(1)}, f32[3,32,128]{2,1,0:T(8,128)S(1)}, f32[3,128,128]{2,1,0:T(8,128)S(1)}, f32[128,128]{1,0:T(8,128)S(1)}) custom-call(f32[3,32,128]{2,1,0:T(8,128)S(1)} %bitcast.34, f32[3,32,128]{2,1,0:T(8,128)S(1)} %bitcast.35, f32[32,128]{1,0:T(8,128)S(1)} %bitcast.40, f32[32,128]{1,0:T(8,128)S(1)} %bitcast.41, ...), custom_call_target="tpu_custom_call" | custom-call | tf_op jit(solution)/shard_map/pallas_call | solution.py:364
  73.8 0.6 copy.23
  74.4 0.6 copy.24
  75.0 0.7 copy.25
  75.7 0.6 copy.26
  (3 shorter events, 0.0 us)
Async XLA Ops:
  0.6 0.7 copy-start.9
  0.6 1.5 %copy-start.8 = (s32[1,32]{1,0:T(1,128)S(1)}, s32[1,32]{1,0:T(1,128)}, u32[]{:S(2)}) copy-start(s32[1,32]{1,0:T(1,128)} %param.19) | copy-start | bytes 388
  1.3 0.7 copy-start.6
  1.3 0.7 copy-start.7
  1.3 0.9 %copy-start.4 = (f32[1,32,128]{2,1,0:T(8,128)S(1)}, f32[1,32,128]{2,1,0:T(8,128)}, u32[]{:S(2)}) copy-start(f32[1,32,128]{2,1,0:T(8,128)} %param.13) | copy-start | bytes 49156
  1.3 0.9 %copy-start.5 = (f32[1,32,128]{2,1,0:T(8,128)S(1)}, f32[1,32,128]{2,1,0:T(8,128)}, u32[]{:S(2)}) copy-start(f32[1,32,128]{2,1,0:T(8,128)} %param.14) | copy-start | bytes 49156
  2.2 1.2 %copy-start = (bf16[1,32,128,128]{3,2,1,0:T(8,128)(2,1)S(1)}, bf16[1,32,128,128]{3,2,1,0:T(8,128)(2,1)}, u32[]{:S(2)}) copy-start(bf16[1,32,128,128]{3,2,1,0:T(8,128)(2,1)} %param.20) | copy-start | bytes 3145732
  3.5 0.9 %copy-start.1 = (f32[1,128,3,128]{3,1,2,0:T(8,128)S(1)}, f32[1,128,3,128]{3,1,2,0:T(8,128)}, u32[]{:S(2)}) copy-start(f32[1,128,3,128]{3,1,2,0:T(8,128)} %param.21) | copy-start | bytes 589828
  4.4 0.8 %copy-start.2 = (f32[1,32,3,128]{3,1,2,0:T(8,128)S(1)}, f32[1,32,3,128]{3,1,2,0:T(8,128)}, u32[]{:S(2)}) copy-start(f32[1,32,3,128]{3,1,2,0:T(8,128)} %param.11) | copy-start | bytes 147460
  5.2 0.8 %copy-start.3 = (f32[1,32,3,128]{3,1,2,0:T(8,128)S(1)}, f32[1,32,3,128]{3,1,2,0:T(8,128)}, u32[]{:S(2)}) copy-start(f32[1,32,3,128]{3,1,2,0:T(8,128)} %param.12) | copy-start | bytes 147460

commit v3 on v2

--- a/solution.py
+++ b/solution.py
@@ -79,11 +79,12 @@
 
 def kernel(
     bis, dom, pmax,
-    pos_ref, vel_ref, rad_ref, drag_ref, slots_ref, inv_ref, pairs_ref, left_ref, cnt_ref, own_ref, w_hbm, fluid_ref,
+    pos_hbm, vel_hbm, rad_hbm, drag_hbm, slots_ref, inv_ref, pairs_ref, left_ref, cnt_ref, own_ref, w_hbm, fluid_hbm,
     pos_out, vel_out, fluid_out, void_out,
+    pos_ref, vel_ref, rad_ref, drag_ref, fluid_ref,
     st0, st1, mig_s, mig_r, halo_r, own_s, own_r, fl_s, fl_r, w_v, flrow, samp,
-    a_ref, xb_ref, b_ref, f_ref, sel_ref, oh_ref, dep, dep_s, dep_r,
-    w_sem, mig_ss, mig_rs, halo_ss, halo_rs, own_ss, own_rs, fl_ss, fl_rs, dep_ss, dep_rs,
+    a_ref, xb_ref, b_ref, f_ref, sel_ref, oh_ref, dep, mass_s, mass_r, da, db,
+    in_sem, w_sem, mig_ss, mig_rs, halo_ss, halo_rs, own_ss, own_rs, fl_ss, fl_rs, mass_ss, mass_rs, dep_ss, dep_rs,
 ):
     nb = st0.shape[0]
     per = BLK // nb
@@ -92,9 +93,6 @@
     mine = lax.axis_index("dom")
     right, left = lax.rem(mine + 1, dom), lax.rem(mine + dom - 1, dom)
 
-    weights_copy = pltpu.make_async_copy(w_hbm, w_v, w_sem)
-    weights_copy.start()
-
     barrier = pltpu.get_barrier_semaphore()
 
     def greet(r, _):
@@ -104,6 +102,17 @@
     lax.fori_loop(1, bis, greet, 0)
     for side in (left, right):
         pl.semaphore_signal(barrier, inc=1, device_id={"dom": side}, device_id_type=MESH)
+
+    inputs = [
+        pltpu.make_async_copy(src, dst, in_sem.at[k])
+        for k, (src, dst) in enumerate((
+            (pos_hbm, pos_ref), (vel_hbm, vel_ref), (rad_hbm, rad_ref), (drag_hbm, drag_ref), (fluid_hbm, fluid_ref)
+        ))
+    ]
+    for copy in inputs:
+        copy.start()
+    weights_copy = pltpu.make_async_copy(w_hbm, w_v, w_sem)
+    weights_copy.start()
 
     def to_peer(r, source, target, ss, rs):
         peer = lax.rem(me + r, bis)
@@ -126,14 +135,22 @@
 
         lax.fori_loop(1, bis, step, 0)
 
+    own_s[...] = jnp.zeros((8, BLK), jnp.int32)
+    own_s[:, 0:nb] = jnp.broadcast_to(own_ref[...], (8, nb))
+    lane8 = lax.broadcasted_iota(jnp.int32, (8, BLK), 1)
+    quarter = lax.rem(me, per)
+    half = nb // 2
+    owners = own_s[...]
+    low = pltpu.roll(jnp.where(lane8 < half, owners, 0), half * quarter, 1)
+    high = pltpu.roll(jnp.where((lane8 >= half) & (lane8 < nb), owners, 0), BLK // 2 - half + half * quarter, 1)
+    own_s[...] = low + high
+    for copy in inputs[:4]:
+        copy.wait()
     for k in range(3):
         st0[:, k, :] = pos_ref[k]
         st0[:, 3 + k, :] = vel_ref[k]
     st0[:, 6, :] = rad_ref[...]
     st0[:, 7, :] = drag_ref[...]
-    lane8 = lax.broadcasted_iota(jnp.int32, (8, BLK), 1)
-    quarter = lax.rem(me, per)
-    own_s[...] = jnp.where(lane8 // nb == quarter, own_ref[...], 0)
     own_r[me] = own_s[...]
 
     capacity = mig_s.shape[1]
@@ -178,6 +195,7 @@
     migrate_copy(1).start()
 
     wait_all(own_source, own_r, own_ss, own_rs)
+    inputs[4].wait()
     fluid_bf = jnp.concatenate([fluid_ref[k].astype(BF16) for k in range(3)], axis=1)
     rows = []
     for t in range(tiles):
@@ -191,7 +209,9 @@
         oh_ref[t] = hot.astype(BF16)
         chosen = jnp.dot(hot.T.astype(BF16), fluid_bf, preferred_element_type=F32).astype(BF16)
         for i in range(per):
-            fl_s[per * t + i] = chosen[nb * i:nb * (i + 1)]
+            for h in range(2):
+                first_row = BLK // 2 * h + half * i
+                fl_s[per * t + i, half * h:half * (h + 1)] = chosen[first_row:first_row + half]
     fl_r[me] = fl_s[me]
 
     migrate_copy(1).wait()
@@ -224,6 +244,32 @@
         for c in range(4):
             xb_ref[j, c] = wide[:, c * BLK:(c + 1) * BLK]
 
+    mass_source = lambda peer: mass_s
+
+    def deposit(n, _):
+        dep[n] = jnp.dot(flrow[n].astype(BF16), w_v[n], preferred_element_type=F32)
+        return 0
+
+    def deposit_mass():
+        flrow[...] = jnp.zeros(flrow.shape, F32)
+        flrow[:, 0, :] = (st0[:, 6, :] / RADIUS_REF) ** 3
+        weights_copy.wait()
+        lax.fori_loop(0, nb, deposit, 0, unroll=8)
+        mass_s[...] = dep[:, 0, :]
+        mass_r[me] = mass_s[...]
+        start_all(mass_source, mass_r, mass_ss, mass_rs)
+
+    def solid_volume():
+        wait_all(mass_source, mass_r, mass_ss, mass_rs)
+        solid = jnp.zeros((BLK, BLK), F32)
+        for t in range(tiles):
+            values = jnp.concatenate([
+                mass_r[per * t:per * (t + 1), half * h:half * (h + 1)].reshape(BLK // 2, BLK) for h in range(2)
+            ], axis=0)
+            for piece in split(values)[::-1]:
+                solid = solid + jnp.dot(oh_ref[t], piece.astype(BF16), preferred_element_type=F32)
+        void_out[...] = 1.0 / (1.0 + solid)
+
     def contacts(step, state):
         for copy in halo_copies(step, state):
             copy.start()
@@ -237,6 +283,10 @@
             return 0
 
         lax.fori_loop(0, nb, own_blocks, 0, unroll=4)
+        if step == 0:
+            deposit_mass()
+        if step == 1:
+            solid_volume()
         for copy in halo_copies(step, state):
             copy.wait()
 
@@ -264,7 +314,7 @@
         lax.fori_loop(0, pmax, pair, 0, unroll=min(16, pmax))
         lane = lax.broadcasted_iota(jnp.int32, (nb, pmax), 1)
         blk_id = lax.broadcasted_iota(jnp.int32, (nb, pmax), 0)
-        hot = jnp.where((left_ref[...] == blk_id) & (lane < cnt_ref[0, 0]), 1.0, 0.0).astype(BF16)
+        hot = jnp.where((left_ref[0:1] == blk_id) & (lane < cnt_ref[0, 0]), 1.0, 0.0).astype(BF16)
         out = []
         for k in range(3):
             acc = jnp.zeros((nb, BLK), F32)
@@ -278,10 +328,8 @@
         total = fl_r[0].astype(F32)
         for g in range(1, bis):
             total = total + fl_r[g].astype(F32)
-        flrow[...] = jnp.zeros(flrow.shape, F32)
         for k in range(3):
             flrow[:, k, :] = total[:, k * BLK:(k + 1) * BLK]
-        weights_copy.wait()
 
         def step(n, _):
             samp[n] = lax.dot_general(
@@ -316,34 +364,82 @@
         pos_out[k] = place[k]
         vel_out[k] = speed[k]
 
-    flrow[...] = jnp.zeros(flrow.shape, F32)
+    ring = 4
+    cols = bis // ring
+    my_y, my_z = me // ring, lax.rem(me, ring)
+    steps_z = (1, 3, 2)
+    steps_y = (1, 3, 2)[:cols - 1] if cols > 2 else (1,)
+    along_z = lambda i: my_y * ring + lax.rem(my_z + i, ring)
+    along_y = lambda i: lax.rem(my_y + i, cols) * ring + my_z
+
+    def relay(h, slot, sem, peer):
+        buffer = (da, db)[h]
+        return pltpu.make_async_remote_copy(
+            src_ref=buffer.at[slot], dst_ref=buffer.at[slot], send_sem=dep_ss.at[h, sem], recv_sem=dep_rs.at[h, slot],
+            device_id={"bis": peer}, device_id_type=MESH,
+        )
+
     for k in range(3):
         flrow[:, k, :] = (masses * beta) * (sampled[k] - speed[k])
-    flrow[:, 3, :] = masses
-
-    def deposit(n, _):
-        dep[n] = jnp.dot(flrow[n].astype(BF16), w_v[n], preferred_element_type=F32)
-        return 0
-
-    lax.fori_loop(0, nb, deposit, 0, unroll=8)
-    for k in range(4):
-        dep_s[k] = dep[:, k, :]
-    dep_source = lambda peer: dep_s
-    start_all(dep_source, dep_r, dep_ss, dep_rs)
-    dep_r[me] = dep_s[...]
-    wait_all(dep_source, dep_r, dep_ss, dep_rs)
-    totals = []
-    for k in (3, 0, 1, 2):
+    sent = []
+
+    def send(h, slot, peer):
+        copy = relay(h, slot, sum(1 for g, _ in sent if g == h), peer)
+        copy.start()
+        sent.append((h, copy))
+
+    routes = ((along_z, steps_z, along_y, steps_y), (along_y, steps_y, along_z, steps_z))
+    for h in range(2):
+        lax.fori_loop(half * h, half * (h + 1), deposit, 0, unroll=8)
+        buffer = (da, db)[h]
+        for k in range(3):
+            buffer[me, k] = dep[half * h:half * (h + 1), k, :]
+        first, steps, _, _ = routes[h]
+        for i in steps:
+            send(h, me, first(i))
+    for h in range(2):
+        _, _, second, steps = routes[h]
+        for i in steps:
+            send(h, me, second(i))
+    for h, i in [(h, i) for i in range(3) for h in range(2)]:
+        first, steps, second, others = routes[h]
+        if i >= len(steps):
+            continue
+        slot = first(-steps[i] + (ring if h == 0 else cols))
+        relay(h, slot, 0, lax.rem(me + 1, bis)).wait_recv()
+        for i in others:
+            send(h, slot, second(i))
+    for y in range(1, cols):
+        for z in range(ring):
+            relay(0, lax.rem(my_y + y, cols) * ring + z, 0, lax.rem(me + 1, bis)).wait_recv()
+    for y in range(cols):
+        for z in range(1, ring):
+            relay(1, y * ring + lax.rem(my_z + z, ring), 0, lax.rem(me + 1, bis)).wait_recv()
+
+    def reduce(values_of):
         acc = jnp.zeros((BLK, BLK), F32)
         for t in range(tiles):
-            values = dep_r[per * t:per * (t + 1), k].reshape(BLK, BLK)
+            values = jnp.concatenate([values_of(t, h).reshape(BLK // 2, BLK) for h in range(2)], axis=0)
             for piece in split(values)[::-1]:
                 acc = acc + jnp.dot(oh_ref[t], piece.astype(BF16), preferred_element_type=F32)
-        totals.append(acc)
-    void = 1.0 / (1.0 + totals[0])
-    void_out[...] = void
+        return acc
+
+    void = void_out[...]
     for k in range(3):
-        fluid_out[k] = fluid_ref[k] - FLUID_GAIN * totals[1 + k] * void
+        total = reduce(lambda t, h: (da, db)[h][per * t:per * (t + 1), k])
+        fluid_out[k] = fluid_ref[k] - FLUID_GAIN * total * void
+    for _, copy in sent:
+        copy.wait_send()
+
+
+def copy_out(*refs):
+    sem = refs[-1]
+    count = len(refs) // 2
+    copies = [pltpu.make_async_copy(refs[k], refs[count + k], sem.at[k]) for k in range(count)]
+    for copy in copies:
+        copy.start()
+    for copy in copies:
+        copy.wait()
 
 
 def local(
@@ -359,6 +455,7 @@
     inverse = jnp.max(jnp.where(hit, j[None, None, :], -1), axis=2)
     vmem = pl.BlockSpec(memory_space=pltpu.VMEM)
     smem = pl.BlockSpec(memory_space=pltpu.SMEM)
+    hbm = pl.BlockSpec(memory_space=pl.ANY)
     dma = pltpu.SemaphoreType.DMA
     tiles = bis * nb // BLK
     outs = pl.pallas_call(
@@ -369,9 +466,14 @@
             jax.ShapeDtypeStruct((3, fb, BLK), F32),
             jax.ShapeDtypeStruct((fb, BLK), F32),
         ),
-        in_specs=[vmem] * 4 + [smem] * 3 + [vmem, smem, vmem, pl.BlockSpec(memory_space=pl.ANY), vmem],
+        in_specs=[hbm] * 4 + [smem] * 3 + [vmem, smem, vmem, hbm, hbm],
         out_specs=(vmem,) * 4,
         scratch_shapes=[
+            pltpu.VMEM((3, nb, BLK), F32),
+            pltpu.VMEM((3, nb, BLK), F32),
+            pltpu.VMEM((nb, BLK), F32),
+            pltpu.VMEM((nb, BLK), F32),
+            pltpu.VMEM((3, fb, BLK), F32),
             pltpu.VMEM((nb, 8, BLK), F32),
             pltpu.VMEM((nb, 8, BLK), F32),
             pltpu.VMEM((levels, capacity, 8, BLK), F32),
@@ -391,8 +493,11 @@
             pltpu.VMEM((64, 4 * BLK), BF16),
             pltpu.VMEM((tiles, BLK, BLK), BF16),
             pltpu.VMEM((nb, 8, BLK), F32),
-            pltpu.VMEM((4, nb, BLK), F32),
-            pltpu.VMEM((bis, 4, nb, BLK), F32),
+            pltpu.VMEM((nb, BLK), F32),
+            pltpu.VMEM((bis, nb, BLK), F32),
+            pltpu.VMEM((bis, 3, nb // 2, BLK), F32),
+            pltpu.VMEM((bis, 3, nb // 2, BLK), F32),
+            dma((5,)),
             dma,
             dma((levels,)),
             dma((levels,)),
@@ -404,6 +509,8 @@
             dma((bis,)),
             dma((bis,)),
             dma((bis,)),
+            dma((2, bis)),
+            dma((2, bis)),
         ],
         compiler_params=pltpu.CompilerParams(
             collective_id=0, has_side_effects=True, vmem_limit_bytes=48 * 1024 * 1024
@@ -416,13 +523,19 @@
         mig_slots[0],
         inverse,
         pair_lists[0],
-        pair_lists[0, 0:1],
+        pair_lists[0],
         pair_counts,
-        jnp.tile(owners, (1, BLK // nb)),
+        owners,
         dep_weights[0],
         jnp.transpose(fluid_velocity[0], (1, 0, 2)),
     )
-    pos, vel, fluid, void = outs
+    pos, vel, fluid, void = pl.pallas_call(
+        copy_out,
+        out_shape=tuple(jax.ShapeDtypeStruct(out.shape, out.dtype) for out in outs),
+        in_specs=[hbm] * 4,
+        out_specs=(hbm,) * 4,
+        scratch_shapes=[dma((4,))],
+    )(*outs)
     return (
         jnp.transpose(pos, (1, 0, 2))[None],
         jnp.transpose(vel, (1, 0, 2))[None],

time: 77.8 us -> 85.7 us (1.10); the launches traced: 76.3 us -> 85.3 us
  Pallas kernels: 67.8 us -> 75.5 us
  local copies, waits for them, and re-layouts: 6.98 us -> 8.19 us
    pallas_call x0 -> x1, Pallas kernels: none -> 12.1 us  [local(): pl.pallas_call(copy_out, out_shape=tuple((jax.ShapeDtypeStruct(out.shape,...]
    pallas_call x1, Pallas kernels: 67.8 us -> 63.5 us  [local(): pl.pallas_call(functools.partial(kernel, bis, dom, pmax), out_shape=(jax....]
    unnamed x25 -> x29, local copies, waits for them, and re-layouts: 6.89 us -> 8.19 us
where the time goes in v3:
time: 85.7 us; the launch traced here: 85.3 us
  Pallas kernels  75.5 us (88%)
  local copies, waits for them, and re-layouts  8.19 us (10%)
  between operations  1.36 us (2%)
    pallas_call x1, Pallas kernels, local(): pl.pallas_call(functools.partial(kernel, bis, dom, pmax), out_shape=(jax....  63.5 us
    pallas_call x1, Pallas kernels, local(): pl.pallas_call(copy_out, out_shape=tuple((jax.ShapeDtypeStruct(out.shape,...  12.1 us
    unnamed x29, local copies, waits for them, and re-layouts  8.19 us

profile of v3, /device:TPU:0, one launch (start us, length us, event | category | flops | bytes accessed | tf_op | source)
XLA Modules:
  0.0 85.3 jit_solution(7729965754885287491)
XLA Ops:
  0.6 0.0 copy-start.8
  1.3 0.0 copy-start.13
  1.3 0.0 copy-start.12
  1.3 0.6 copy-done.13
  2.0 0.1 iota_compare_fusion.1
  2.0 0.0 copy-done.12
  2.0 0.0 copy-start.10
  2.0 0.0 copy-start.11
  2.1 0.1 select_reduce_fusion.inv_ref
  2.1 0.0 copy-done.8
  2.2 0.6 copy-done.10
  2.7 0.0 copy-done.11
  2.7 0.0 copy-start
  2.7 1.2 %copy-done = bf16[1,32,128,128]{3,2,1,0:T(8,128)(2,1)S(1)} copy-done((bf16[1,32,128,128]{3,2,1,0:T(8,128)(2,1)S(1)}, bf16[1,32,128,128]{3,2,1,0:T(8,128)(2,1)}, u32[]{:S(2)}) %copy-start) | copy-done | bytes 1048600
  3.9 0.0 copy-start.1
  3.9 0.9 %copy-done.1 = f32[1,128,3,128]{3,1,2,0:T(8,128)S(1)} copy-done((f32[1,128,3,128]{3,1,2,0:T(8,128)S(1)}, f32[1,128,3,128]{3,1,2,0:T(8,128)}, u32[]{:S(2)}) %copy-start.1) | copy-done | bytes 196632
  4.9 0.0 copy-start.4
  4.9 0.8 copy-done.4
  5.7 0.0 copy-start.5
  5.7 0.8 copy-done.5
  6.5 0.0 copy-start.9
  6.5 0.7 copy-done.9
  7.2 63.5 %shard_map.138 = (f32[3,32,128]{2,1,0:T(8,128)S(1)}, f32[3,32,128]{2,1,0:T(8,128)S(1)}, f32[3,128,128]{2,1,0:T(8,128)S(1)}, f32[128,128]{1,0:T(8,128)S(1)}) custom-call(f32[3,32,128]{2,1,0:T(8,128)S(1)} %bitcast.29, f32[3,32,128]{2,1,0:T(8,128)S(1)} %bitcast.30, f32[32,128]{1,0:T(8,128)S(1)} %bitcast.33, f32[32,128]{1,0:T(8,128)S(1)} %bitcast.34, ...), custom_call_target="tpu_custom_call" | custom-call | tf_op jit(solution)/shard_map/pallas_call | solution.py:461
  70.7 0.0 copy-start.2
  70.7 0.7 copy-done.2
  71.4 0.0 copy-start.3
  71.4 0.6 copy-done.3
  72.0 0.0 copy-start.6
  72.0 0.6 copy-done.6
  72.6 0.0 copy-start.7
  72.6 0.6 copy-done.7
  73.2 12.1 %shard_map.139 = (f32[3,32,128]{2,1,0:T(8,128)}, f32[3,32,128]{2,1,0:T(8,128)}, f32[3,128,128]{2,1,0:T(8,128)}, f32[128,128]{1,0:T(8,128)}) custom-call(f32[3,32,128]{2,1,0:T(8,128)} %copy-done.6, f32[3,32,128]{2,1,0:T(8,128)} %copy-done.7, f32[3,128,128]{2,1,0:T(8,128)} %copy-done.2, f32[128,128]{1,0:T(8,128)} %copy-done.3), custom_call_target="tpu_custom_call" | custom-call | tf_op jit(solution)/shard_map/pallas_call | solution.py:532
  (1 shorter events, 0.0 us)
Async XLA Ops:
  0.6 1.5 %copy-start.8 = (f32[1,32,128]{2,1,0:T(8,128)S(1)}, f32[1,32,128]{2,1,0:T(8,128)}, u32[]{:S(2)}) copy-start(f32[1,32,128]{2,1,0:T(8,128)} %param.13) | copy-start | bytes 49156
  1.3 0.7 copy-start.13
  1.3 0.7 copy-start.12
  2.0 0.7 copy-start.10
  2.0 0.7 copy-start.11
  2.7 1.2 %copy-start = (bf16[1,32,128,128]{3,2,1,0:T(8,128)(2,1)S(1)}, bf16[1,32,128,128]{3,2,1,0:T(8,128)(2,1)}, u32[]{:S(2)}) copy-start(bf16[1,32,128,128]{3,2,1,0:T(8,128)(2,1)} %param.20) | copy-start | bytes 3145732
  3.9 0.9 %copy-start.1 = (f32[1,128,3,128]{3,1,2,0:T(8,128)S(1)}, f32[1,128,3,128]{3,1,2,0:T(8,128)}, u32[]{:S(2)}) copy-start(f32[1,128,3,128]{3,1,2,0:T(8,128)} %param.21) | copy-start | bytes 589828
  4.9 0.8 copy-start.4
  5.7 0.8 copy-start.5
  6.5 0.7 copy-start.9
  70.7 0.7 copy-start.2
  71.4 0.6 copy-start.3
  72.0 0.6 copy-start.6
  72.6 0.6 copy-start.7

commit v4 on v3

--- a/solution.py
+++ b/solution.py
@@ -79,12 +79,12 @@
 
 def kernel(
     bis, dom, pmax,
-    pos_hbm, vel_hbm, rad_hbm, drag_hbm, slots_ref, inv_ref, pairs_ref, left_ref, cnt_ref, own_ref, w_hbm, fluid_hbm,
+    pos_hbm, vel_hbm, rad_hbm, drag_hbm, slots_ref, moved_ref, pairs_ref, cnt_ref, left_hbm, own_hbm, w_hbm, fluid_hbm,
     pos_out, vel_out, fluid_out, void_out,
-    pos_ref, vel_ref, rad_ref, drag_ref, fluid_ref,
+    pos_ref, vel_ref, rad_ref, drag_ref, left_ref, own_ref, fluid_ref, inv_v, inv_ref,
     st0, st1, mig_s, mig_r, halo_r, own_s, own_r, fl_s, fl_r, w_v, flrow, samp,
     a_ref, xb_ref, b_ref, f_ref, sel_ref, oh_ref, dep, mass_s, mass_r, da, db,
-    in_sem, w_sem, mig_ss, mig_rs, halo_ss, halo_rs, own_ss, own_rs, fl_ss, fl_rs, mass_ss, mass_rs, dep_ss, dep_rs,
+    in_sem, inv_sem, w_sem, mig_ss, mig_rs, halo_ss, halo_rs, own_ss, own_rs, fl_ss, fl_rs, mass_ss, mass_rs, dep_ss, dep_rs,
 ):
     nb = st0.shape[0]
     per = BLK // nb
@@ -106,7 +106,8 @@
     inputs = [
         pltpu.make_async_copy(src, dst, in_sem.at[k])
         for k, (src, dst) in enumerate((
-            (pos_hbm, pos_ref), (vel_hbm, vel_ref), (rad_hbm, rad_ref), (drag_hbm, drag_ref), (fluid_hbm, fluid_ref)
+            (pos_hbm, pos_ref), (vel_hbm, vel_ref), (rad_hbm, rad_ref), (drag_hbm, drag_ref),
+            (own_hbm, own_ref), (left_hbm, left_ref), (fluid_hbm, fluid_ref),
         ))
     ]
     for copy in inputs:
@@ -135,25 +136,32 @@
 
         lax.fori_loop(1, bis, step, 0)
 
+    lane8 = lax.broadcasted_iota(jnp.int32, (8, BLK), 1)
+    capacity = mig_s.shape[1]
+    places = jnp.full((8, BLK), -1, jnp.int32)
+    for level in range(mig_s.shape[0]):
+        for j in range(capacity):
+            here = (lane8 == slots_ref[level, j]) & (row_ids() == level) & (moved_ref[0, level] > j)
+            places = jnp.where(here, j, places)
+    inv_v[...] = places
+    inv_copy = pltpu.make_async_copy(inv_v, inv_ref, inv_sem)
+    inv_copy.start()
+    for copy in inputs[:6]:
+        copy.wait()
     own_s[...] = jnp.zeros((8, BLK), jnp.int32)
     own_s[:, 0:nb] = jnp.broadcast_to(own_ref[...], (8, nb))
-    lane8 = lax.broadcasted_iota(jnp.int32, (8, BLK), 1)
     quarter = lax.rem(me, per)
     half = nb // 2
     owners = own_s[...]
     low = pltpu.roll(jnp.where(lane8 < half, owners, 0), half * quarter, 1)
     high = pltpu.roll(jnp.where((lane8 >= half) & (lane8 < nb), owners, 0), BLK // 2 - half + half * quarter, 1)
     own_s[...] = low + high
-    for copy in inputs[:4]:
-        copy.wait()
     for k in range(3):
         st0[:, k, :] = pos_ref[k]
         st0[:, 3 + k, :] = vel_ref[k]
     st0[:, 6, :] = rad_ref[...]
     st0[:, 7, :] = drag_ref[...]
     own_r[me] = own_s[...]
-
-    capacity = mig_s.shape[1]
 
     def gather(level):
         def step(j, _):
@@ -180,6 +188,7 @@
         lax.fori_loop(0, nb, step, 0, unroll=4)
 
     gather(0)
+    inv_copy.wait()
     pl.semaphore_wait(barrier, bis - 1 + 2)
     migrate_copy(0).start()
     own_source = lambda peer: own_s
@@ -195,7 +204,7 @@
     migrate_copy(1).start()
 
     wait_all(own_source, own_r, own_ss, own_rs)
-    inputs[4].wait()
+    inputs[6].wait()
     fluid_bf = jnp.concatenate([fluid_ref[k].astype(BF16) for k in range(3)], axis=1)
     rows = []
     for t in range(tiles):
@@ -449,13 +458,9 @@
     levels, capacity = mig_slots.shape[1:]
     pmax = pair_lists.shape[2]
     fb = fluid_velocity.shape[1]
-    j = jnp.arange(capacity, dtype=jnp.int32)
-    hit = mig_slots[0][:, None, :] == jnp.arange(nb, dtype=jnp.int32)[None, :, None]
-    hit = hit & (j[None, None, :] < mig_counts[0][:, None, None])
-    inverse = jnp.max(jnp.where(hit, j[None, None, :], -1), axis=2)
     vmem = pl.BlockSpec(memory_space=pltpu.VMEM)
     smem = pl.BlockSpec(memory_space=pltpu.SMEM)
-    hbm = pl.BlockSpec(memory_space=pl.ANY)
+    hbm = pl.BlockSpec(memory_space=pltpu.HBM)
     dma = pltpu.SemaphoreType.DMA
     tiles = bis * nb // BLK
     outs = pl.pallas_call(
@@ -466,14 +471,18 @@
             jax.ShapeDtypeStruct((3, fb, BLK), F32),
             jax.ShapeDtypeStruct((fb, BLK), F32),
         ),
-        in_specs=[hbm] * 4 + [smem] * 3 + [vmem, smem, vmem, hbm, hbm],
+        in_specs=[hbm] * 4 + [smem] * 4 + [hbm] * 4,
         out_specs=(vmem,) * 4,
         scratch_shapes=[
             pltpu.VMEM((3, nb, BLK), F32),
             pltpu.VMEM((3, nb, BLK), F32),
             pltpu.VMEM((nb, BLK), F32),
             pltpu.VMEM((nb, BLK), F32),
+            pltpu.VMEM((2, pmax), jnp.int32),
+            pltpu.VMEM((1, nb), jnp.int32),
             pltpu.VMEM((3, fb, BLK), F32),
+            pltpu.VMEM((8, BLK), jnp.int32),
+            pltpu.SMEM((8, BLK), jnp.int32),
             pltpu.VMEM((nb, 8, BLK), F32),
             pltpu.VMEM((nb, 8, BLK), F32),
             pltpu.VMEM((levels, capacity, 8, BLK), F32),
@@ -497,7 +506,8 @@
             pltpu.VMEM((bis, nb, BLK), F32),
             pltpu.VMEM((bis, 3, nb // 2, BLK), F32),
             pltpu.VMEM((bis, 3, nb // 2, BLK), F32),
-            dma((5,)),
+            dma((7,)),
+            dma,
             dma,
             dma((levels,)),
             dma((levels,)),
@@ -513,7 +523,7 @@
             dma((2, bis)),
         ],
         compiler_params=pltpu.CompilerParams(
-            collective_id=0, has_side_effects=True, vmem_limit_bytes=48 * 1024 * 1024
+            collective_id=0, has_side_effects=True, vmem_limit_bytes=64 * 1024 * 1024
         ),
     )(
         jnp.transpose(positions[0], (1, 0, 2)),
@@ -521,10 +531,10 @@
         radii[0],
         drag_rates[0],
         mig_slots[0],
-        inverse,
-        pair_lists[0],
+        mig_counts,
         pair_lists[0],
         pair_counts,
+        pair_lists[0],
         owners,
         dep_weights[0],
         jnp.transpose(fluid_velocity[0], (1, 0, 2)),
@@ -532,9 +542,10 @@
     pos, vel, fluid, void = pl.pallas_call(
         copy_out,
         out_shape=tuple(jax.ShapeDtypeStruct(out.shape, out.dtype) for out in outs),
-        in_specs=[hbm] * 4,
+        in_specs=[vmem] * 4,
         out_specs=(hbm,) * 4,
         scratch_shapes=[dma((4,))],
+        compiler_params=pltpu.CompilerParams(vmem_limit_bytes=64 * 1024 * 1024),
     )(*outs)
     return (
         jnp.transpose(pos, (1, 0, 2))[None],

time: 85.7 us -> 69.2 us (0.81)
  Pallas kernels: 75.5 us -> 66.4 us
  local copies, waits for them, and re-layouts: 8.19 us -> 1.25 us
    pallas_call x1, Pallas kernels: 12.1 us -> 1.75 us  [local(): pl.pallas_call(copy_out, out_shape=tuple((jax.ShapeDtypeStruct(out.shape,...]
    unnamed x29 -> x3, local copies, waits for them, and re-layouts: 8.19 us -> 1.25 us
    pallas_call x1, Pallas kernels: 63.5 us -> 64.7 us  [local(): pl.pallas_call(functools.partial(kernel, bis, dom, pmax), out_shape=(jax....]
where the time goes in v4:
time: 69.2 us; the launch traced here: 69 us
  Pallas kernels  66.4 us (96%)
  between operations  1.29 us (2%)
  local copies, waits for them, and re-layouts  1.25 us (2%)
    pallas_call x1, Pallas kernels, local(): pl.pallas_call(functools.partial(kernel, bis, dom, pmax), out_shape=(jax....  64.7 us
    pallas_call x1, Pallas kernels, local(): pl.pallas_call(copy_out, out_shape=tuple((jax.ShapeDtypeStruct(out.shape,...  1.75 us

profile of v4, /device:TPU:0, one launch (start us, length us, event | category | flops | bytes accessed | tf_op | source)
XLA Modules:
  0.0 69.0 jit_solution(6172393855628032043)
XLA Ops:
  1.3 0.0 copy-start
  1.3 0.7 copy-done
  2.0 0.6 copy.17
  2.5 64.7 %shard_map.138 = (f32[3,32,128]{2,1,0:T(8,128)}, f32[3,32,128]{2,1,0:T(8,128)}, f32[3,128,128]{2,1,0:T(8,128)}, f32[128,128]{1,0:T(8,128)}) custom-call(f32[3,32,128]{2,1,0:T(8,128)} %bitcast.28, f32[3,32,128]{2,1,0:T(8,128)} %bitcast.29, f32[32,128]{1,0:T(8,128)} %bitcast.30, f32[32,128]{1,0:T(8,128)} %bitcast.31, s32[3,16]{1,0:T(4,128)} %bitcast.34, ...), custom_call_target="tpu_custom_call" | custom-call | tf_op jit(solution)/shard_map/pallas_call | solution.py:466
  67.2 1.8 %shard_map.139 = (f32[3,32,128]{2,1,0:T(8,128)}, f32[3,32,128]{2,1,0:T(8,128)}, f32[3,128,128]{2,1,0:T(8,128)}, f32[128,128]{1,0:T(8,128)}) custom-call(f32[3,32,128]{2,1,0:T(8,128)} %get-tuple-element.12.refs_0_, f32[3,32,128]{2,1,0:T(8,128)} %get-tuple-element.13.refs_1_, f32[3,128,128]{2,1,0:T(8,128)} %get-tuple-element.14.refs_2_, ...), custom_call_target="tpu_custom_call" | custom-call | tf_op jit(solution)/shard_map/pallas_call | solution.py:542
Async XLA Ops:
  1.3 0.7 copy-start

commit v5 on v4

--- a/solution.py
+++ b/solution.py
@@ -79,12 +79,13 @@
 
 def kernel(
     bis, dom, pmax,
-    pos_hbm, vel_hbm, rad_hbm, drag_hbm, slots_ref, moved_ref, pairs_ref, cnt_ref, left_hbm, own_hbm, w_hbm, fluid_hbm,
-    pos_out, vel_out, fluid_out, void_out,
-    pos_ref, vel_ref, rad_ref, drag_ref, left_ref, own_ref, fluid_ref, inv_v, inv_ref,
-    st0, st1, mig_s, mig_r, halo_r, own_s, own_r, fl_s, fl_r, w_v, flrow, samp,
+    pos_hbm, vel_hbm, rad_hbm, drag_hbm, slots_hbm, moved_hbm, pairs_hbm, cnt_hbm, left_hbm, own_hbm, w_hbm, fluid_hbm,
+    pos_hbm_out, vel_hbm_out, fluid_hbm_out, void_hbm_out,
+    slots_ref, moved_ref, pairs_ref, cnt_ref,
+    pos_out, vel_out, fluid_out, void_out, pos_ref, vel_ref, rad_ref, drag_ref, left_ref, own_ref, fluid_ref, inv_v, inv_ref,
+    st0, st1, mig_s, mig_r, from_s, from_near, from_far, halo_r, own_s, own_r, fl_s, fl_r, w_v, flrow, samp,
     a_ref, xb_ref, b_ref, f_ref, sel_ref, oh_ref, dep, mass_s, mass_r, da, db,
-    in_sem, inv_sem, w_sem, mig_ss, mig_rs, halo_ss, halo_rs, own_ss, own_rs, fl_ss, fl_rs, mass_ss, mass_rs, dep_ss, dep_rs,
+    in_sem, inv_sem, out_sem, w_sem, mig_ss, mig_rs, halo_ss, halo_rs, own_ss, own_rs, fl_ss, fl_rs, mass_ss, mass_rs, dep_ss, dep_rs,
 ):
     nb = st0.shape[0]
     per = BLK // nb
@@ -108,6 +109,7 @@
         for k, (src, dst) in enumerate((
             (pos_hbm, pos_ref), (vel_hbm, vel_ref), (rad_hbm, rad_ref), (drag_hbm, drag_ref),
             (own_hbm, own_ref), (left_hbm, left_ref), (fluid_hbm, fluid_ref),
+            (slots_hbm, slots_ref), (moved_hbm, moved_ref), (pairs_hbm, pairs_ref), (cnt_hbm, cnt_ref),
         ))
     ]
     for copy in inputs:
@@ -136,10 +138,12 @@
 
         lax.fori_loop(1, bis, step, 0)
 
+    for copy in inputs[7:]:
+        copy.wait()
     lane8 = lax.broadcasted_iota(jnp.int32, (8, BLK), 1)
-    capacity = mig_s.shape[1]
+    capacity = slots_ref.shape[1]
     places = jnp.full((8, BLK), -1, jnp.int32)
-    for level in range(mig_s.shape[0]):
+    for level in range(slots_ref.shape[0]):
         for j in range(capacity):
             here = (lane8 == slots_ref[level, j]) & (row_ids() == level) & (moved_ref[0, level] > j)
             places = jnp.where(here, j, places)
@@ -163,34 +167,72 @@
     st0[:, 7, :] = drag_ref[...]
     own_r[me] = own_s[...]
 
-    def gather(level):
+    def gather(level, target):
         def step(j, _):
-            mig_s[level, j] = st0[slots_ref[level, j]]
-            return 0
-
-        lax.fori_loop(0, capacity, step, 0, unroll=4)
-
-    def migrate_copy(level):
+            target[j] = st0[slots_ref[level, j]]
+            return 0
+
+        lax.fori_loop(0, capacity, step, 0, unroll=8)
+
+    def flip(level):
         stride = 2**level
-        bit = lax.rem(me // stride, 2)
-        partner = me + stride - 2 * stride * bit
+        return stride - 2 * stride * lax.rem(me // stride, 2)
+
+    def migrate_copy(k, source, target, partner):
         return pltpu.make_async_remote_copy(
-            src_ref=mig_s.at[level], dst_ref=mig_r[level], send_sem=mig_ss.at[level], recv_sem=mig_rs.at[level],
+            src_ref=source, dst_ref=target, send_sem=mig_ss.at[k], recv_sem=mig_rs.at[k],
             device_id={"bis": partner}, device_id_type=MESH,
         )
 
-    def scatter(level):
+    def scatter(level, arrived):
         def step(n, _):
             j = inv_ref[level, n]
-            st0[n] = jnp.where(j >= 0, mig_r[level][jnp.maximum(j, 0)], st0[n])
-            return 0
-
-        lax.fori_loop(0, nb, step, 0, unroll=4)
-
-    gather(0)
+            st0[n] = jnp.where(j >= 0, arrived[jnp.maximum(j, 0)], st0[n])
+            return 0
+
+        lax.fori_loop(0, nb, step, 0, unroll=8)
+
+    near, far = me + flip(1), me + flip(2)
+    both = far + flip(1)
+    level0 = migrate_copy(0, mig_s[0], mig_r[0], me + flip(0))
+    table_near = migrate_copy(1, from_s, from_near, near)
+    table_far = migrate_copy(2, from_s, from_far, far)
+    level1 = migrate_copy(3, mig_s[1], mig_r[1], near)
+    level2 = migrate_copy(4, mig_s[2], mig_r[2], far)
+    level12 = migrate_copy(5, mig_s[3], mig_r[3], both)
+
+    def make_table():
+        row = lax.broadcasted_iota(jnp.int32, (capacity, BLK), 0)
+        table = jnp.zeros((capacity, BLK), jnp.int32)
+        for j in range(capacity):
+            table = jnp.where(row == j, inv_ref[1, slots_ref[2, j]], table)
+        from_s[...] = table
+
+    def pick_for_both():
+        def step(j, _):
+            want = from_near[pl.ds(j, 1), :]
+            block = jnp.zeros((8, BLK), F32)
+            for k in range(capacity):
+                block = jnp.where(want == k, mig_s[1][k], block)
+            mig_s[3][j] = block
+            return 0
+
+        lax.fori_loop(0, capacity, step, 0, unroll=4)
+
+    def merge_level2():
+        def step(j, _):
+            mig_r[2][j] = jnp.where(from_far[pl.ds(j, 1), :] >= 0, mig_r[3][j], mig_r[2][j])
+            return 0
+
+        lax.fori_loop(0, capacity, step, 0, unroll=8)
+
+    gather(0, mig_s[0])
     inv_copy.wait()
+    make_table()
     pl.semaphore_wait(barrier, bis - 1 + 2)
-    migrate_copy(0).start()
+    level0.start()
+    table_near.start()
+    table_far.start()
     own_source = lambda peer: own_s
     start_all(own_source, own_r, own_ss, own_rs)
     srow = lax.broadcasted_iota(jnp.int32, (64, BLK), 0)
@@ -198,10 +240,15 @@
     first = (srow // 8 == 1) | (srow // 8 == 4) | (srow // 8 == 6)
     for c, ch in enumerate((0, 1, 2, 7)):
         sel_ref[:, c * BLK:(c + 1) * BLK] = jnp.where(first & part & (lax.rem(srow, 8) == ch), 1.0, 0.0).astype(BF16)
-    migrate_copy(0).wait()
-    scatter(0)
-    gather(1)
-    migrate_copy(1).start()
+    level0.wait()
+    scatter(0, mig_r[0])
+    gather(1, mig_s[1])
+    level1.start()
+    gather(2, mig_s[2])
+    level2.start()
+    table_near.wait()
+    pick_for_both()
+    level12.start()
 
     wait_all(own_source, own_r, own_ss, own_rs)
     inputs[6].wait()
@@ -223,12 +270,13 @@
                 fl_s[per * t + i, half * h:half * (h + 1)] = chosen[first_row:first_row + half]
     fl_r[me] = fl_s[me]
 
-    migrate_copy(1).wait()
-    scatter(1)
-    gather(2)
-    migrate_copy(2).start()
-    migrate_copy(2).wait()
-    scatter(2)
+    level1.wait()
+    scatter(1, mig_r[1])
+    table_far.wait()
+    level2.wait()
+    level12.wait()
+    merge_level2()
+    scatter(2, mig_r[2])
 
     def halo_copies(step, state):
         return [
@@ -246,11 +294,12 @@
 
     fl_source = lambda peer: fl_s.at[peer]
 
-    def prepare(blk, j):
+    def prepare(step, blk, j):
         t = partner_features(blk).T.astype(BF16)
         a_ref[j] = t
-        wide = jnp.dot(t, sel_ref[...], preferred_element_type=F32)
-        for c in range(4):
+        count = 4 - step
+        wide = jnp.dot(t, sel_ref[:, 0:count * BLK], preferred_element_type=F32)
+        for c in range(count):
             xb_ref[j, c] = wide[:, c * BLK:(c + 1) * BLK]
 
     mass_source = lambda peer: mass_s
@@ -275,7 +324,7 @@
             values = jnp.concatenate([
                 mass_r[per * t:per * (t + 1), half * h:half * (h + 1)].reshape(BLK // 2, BLK) for h in range(2)
             ], axis=0)
-            for piece in split(values)[::-1]:
+            for piece in split(values, 2)[::-1]:
                 solid = solid + jnp.dot(oh_ref[t], piece.astype(BF16), preferred_element_type=F32)
         void_out[...] = 1.0 / (1.0 + solid)
 
@@ -287,7 +336,7 @@
 
         def own_blocks(n, _):
             blk = state[n]
-            prepare(blk, n + G)
+            prepare(step, blk, n + G)
             b_ref[n] = local_features(blk)
             return 0
 
@@ -300,8 +349,8 @@
             copy.wait()
 
         def rim(n, _):
-            prepare(halo_r[step, n], n)
-            prepare(halo_r[step, n + G], n + nb + G)
+            prepare(step, halo_r[step, n], n)
+            prepare(step, halo_r[step, n + G], n + nb + G)
             return 0
 
         lax.fori_loop(0, G, rim, 0, unroll=2)
@@ -320,14 +369,14 @@
             ])
             return 0
 
-        lax.fori_loop(0, pmax, pair, 0, unroll=min(16, pmax))
+        lax.fori_loop(0, pmax, pair, 0, unroll=min(32, pmax))
         lane = lax.broadcasted_iota(jnp.int32, (nb, pmax), 1)
         blk_id = lax.broadcasted_iota(jnp.int32, (nb, pmax), 0)
         hot = jnp.where((left_ref[0:1] == blk_id) & (lane < cnt_ref[0, 0]), 1.0, 0.0).astype(BF16)
         out = []
         for k in range(3):
             acc = jnp.zeros((nb, BLK), F32)
-            for piece in split(f_ref[:, k, :])[::-1]:
+            for piece in split(f_ref[:, k, :], 2)[::-1]:
                 acc = acc + jnp.dot(hot, piece.astype(BF16), preferred_element_type=F32)
             out.append(acc)
         return out
@@ -372,6 +421,15 @@
     for k in range(3):
         pos_out[k] = place[k]
         vel_out[k] = speed[k]
+    results = [
+        pltpu.make_async_copy(src, dst, out_sem.at[k])
+        for k, (src, dst) in enumerate(
+            [(pos_out, pos_hbm_out), (vel_out, vel_hbm_out), (void_out, void_hbm_out)]
+            + [(fluid_out.at[k], fluid_hbm_out.at[k]) for k in range(3)]
+        )
+    ]
+    for copy in results[:3]:
+        copy.start()
 
     ring = 4
     cols = bis // ring
@@ -429,7 +487,7 @@
         acc = jnp.zeros((BLK, BLK), F32)
         for t in range(tiles):
             values = jnp.concatenate([values_of(t, h).reshape(BLK // 2, BLK) for h in range(2)], axis=0)
-            for piece in split(values)[::-1]:
+            for piece in split(values, 2)[::-1]:
                 acc = acc + jnp.dot(oh_ref[t], piece.astype(BF16), preferred_element_type=F32)
         return acc
 
@@ -437,8 +495,11 @@
     for k in range(3):
         total = reduce(lambda t, h: (da, db)[h][per * t:per * (t + 1), k])
         fluid_out[k] = fluid_ref[k] - FLUID_GAIN * total * void
+        results[3 + k].start()
     for _, copy in sent:
         copy.wait_send()
+    for copy in results:
+        copy.wait()
 
 
 def copy_out(*refs):
@@ -471,9 +532,17 @@
             jax.ShapeDtypeStruct((3, fb, BLK), F32),
             jax.ShapeDtypeStruct((fb, BLK), F32),
         ),
-        in_specs=[hbm] * 4 + [smem] * 4 + [hbm] * 4,
-        out_specs=(vmem,) * 4,
+        in_specs=[hbm] * 12,
+        out_specs=(hbm,) * 4,
         scratch_shapes=[
+            pltpu.SMEM((levels, capacity), jnp.int32),
+            pltpu.SMEM((1, levels), jnp.int32),
+            pltpu.SMEM((2, pmax), jnp.int32),
+            pltpu.SMEM((1, 1), jnp.int32),
+            pltpu.VMEM((3, nb, BLK), F32),
+            pltpu.VMEM((3, nb, BLK), F32),
+            pltpu.VMEM((3, fb, BLK), F32),
+            pltpu.VMEM((fb, BLK), F32),
             pltpu.VMEM((3, nb, BLK), F32),
             pltpu.VMEM((3, nb, BLK), F32),
             pltpu.VMEM((nb, BLK), F32),
@@ -485,8 +554,11 @@
             pltpu.SMEM((8, BLK), jnp.int32),
             pltpu.VMEM((nb, 8, BLK), F32),
             pltpu.VMEM((nb, 8, BLK), F32),
-            pltpu.VMEM((levels, capacity, 8, BLK), F32),
-            [pltpu.VMEM((capacity, 8, BLK), F32)] * levels,
+            [pltpu.VMEM((capacity, 8, BLK), F32)] * (levels + 1),
+            [pltpu.VMEM((capacity, 8, BLK), F32)] * (levels + 1),
+            pltpu.VMEM((capacity, BLK), jnp.int32),
+            pltpu.VMEM((capacity, BLK), jnp.int32),
+            pltpu.VMEM((capacity, BLK), jnp.int32),
             pltpu.VMEM((SUBSTEPS, 2 * G, 8, BLK), F32),
             pltpu.VMEM((8, BLK), jnp.int32),
             pltpu.VMEM((bis, 8, BLK), jnp.int32),
@@ -506,11 +578,12 @@
             pltpu.VMEM((bis, nb, BLK), F32),
             pltpu.VMEM((bis, 3, nb // 2, BLK), F32),
             pltpu.VMEM((bis, 3, nb // 2, BLK), F32),
-            dma((7,)),
+            dma((11,)),
             dma,
+            dma((6,)),
             dma,
-            dma((levels,)),
-            dma((levels,)),
+            dma((6,)),
+            dma((6,)),
             dma((SUBSTEPS, 2)),
             dma((SUBSTEPS, 2)),
             dma((bis,)),

time: 69.2 us -> 61.2 us (0.88)
  Pallas kernels: 66.4 us -> 58.5 us
    pallas_call x1, Pallas kernels: 64.7 us -> 56.7 us  [local(): pl.pallas_call(functools.partial(kernel, bis, dom, pmax), out_shape=(jax....]
where the time goes in v5:
time: 61.2 us; the launch traced here: 61 us
  Pallas kernels  58.5 us (96%)
  between operations  1.29 us (2%)
  local copies, waits for them, and re-layouts  1.25 us (2%)
    pallas_call x1, Pallas kernels, local(): pl.pallas_call(functools.partial(kernel, bis, dom, pmax), out_shape=(jax....  56.7 us
    pallas_call x1, Pallas kernels, local(): pl.pallas_call(copy_out, out_shape=tuple((jax.ShapeDtypeStruct(out.shape,...  1.75 us
    unnamed x3, local copies, waits for them, and re-layouts  1.25 us

profile of v5, /device:TPU:0, one launch (start us, length us, event | category | flops | bytes accessed | tf_op | source)
XLA Modules:
  0.0 61.0 jit_solution(7637078483845639279)
XLA Ops:
  1.3 0.0 copy-start
  1.3 0.7 %copy-done = s32[1,3,16]{2,0,1:T(1,128)S(1)} copy-done((s32[1,3,16]{2,0,1:T(1,128)S(1)}, s32[1,3,16]{2,0,1:T(1,128)}, u32[]{:S(2)}) %copy-start) | copy-done | bytes 216
  2.0 0.6 copy.17
  2.5 56.7 %shard_map.138 = (f32[3,32,128]{2,1,0:T(8,128)}, f32[3,32,128]{2,1,0:T(8,128)}, f32[3,128,128]{2,1,0:T(8,128)}, f32[128,128]{1,0:T(8,128)}) custom-call(f32[3,32,128]{2,1,0:T(8,128)} %bitcast.28, f32[3,32,128]{2,1,0:T(8,128)} %bitcast.29, f32[32,128]{1,0:T(8,128)} %bitcast.30, f32[32,128]{1,0:T(8,128)} %bitcast.31, s32[3,16]{1,0:T(4,128)} %bitcast.34, ...), custom_call_target="tpu_custom_call" | custom-call | tf_op jit(solution)/shard_map/pallas_call | solution.py:527
  59.3 1.8 %shard_map.139 = (f32[3,32,128]{2,1,0:T(8,128)}, f32[3,32,128]{2,1,0:T(8,128)}, f32[3,128,128]{2,1,0:T(8,128)}, f32[128,128]{1,0:T(8,128)}) custom-call(f32[3,32,128]{2,1,0:T(8,128)} %get-tuple-element.12.refs_0_, f32[3,32,128]{2,1,0:T(8,128)} %get-tuple-element.13.refs_1_, f32[3,128,128]{2,1,0:T(8,128)} %get-tuple-element.14.refs_2_, ...), custom_call_target="tpu_custom_call" | custom-call | tf_op jit(solution)/shard_map/pallas_call | solution.py:615
Async XLA Ops:
  1.3 0.7 %copy-start = (s32[1,3,16]{2,0,1:T(1,128)S(1)}, s32[1,3,16]{2,0,1:T(1,128)}, u32[]{:S(2)}) copy-start(s32[1,3,16]{2,0,1:T(1,128)} %param.15) | copy-start | bytes 580

commit v6 on v5

--- a/solution.py
+++ b/solution.py
@@ -141,11 +141,11 @@
     for copy in inputs[7:]:
         copy.wait()
     lane8 = lax.broadcasted_iota(jnp.int32, (8, BLK), 1)
-    capacity = slots_ref.shape[1]
+    capacity = slots_ref.shape[2]
     places = jnp.full((8, BLK), -1, jnp.int32)
     for level in range(slots_ref.shape[0]):
         for j in range(capacity):
-            here = (lane8 == slots_ref[level, j]) & (row_ids() == level) & (moved_ref[0, level] > j)
+            here = (lane8 == slots_ref[level, 0, j]) & (row_ids() == level) & (moved_ref[0, level] > j)
             places = jnp.where(here, j, places)
     inv_v[...] = places
     inv_copy = pltpu.make_async_copy(inv_v, inv_ref, inv_sem)
@@ -169,7 +169,7 @@
 
     def gather(level, target):
         def step(j, _):
-            target[j] = st0[slots_ref[level, j]]
+            target[j] = st0[slots_ref[level, 0, j]]
             return 0
 
         lax.fori_loop(0, capacity, step, 0, unroll=8)
@@ -205,7 +205,7 @@
         row = lax.broadcasted_iota(jnp.int32, (capacity, BLK), 0)
         table = jnp.zeros((capacity, BLK), jnp.int32)
         for j in range(capacity):
-            table = jnp.where(row == j, inv_ref[1, slots_ref[2, j]], table)
+            table = jnp.where(row == j, inv_ref[1, slots_ref[2, 0, j]], table)
         from_s[...] = table
 
     def pick_for_both():
@@ -269,6 +269,7 @@
                 first_row = BLK // 2 * h + half * i
                 fl_s[per * t + i, half * h:half * (h + 1)] = chosen[first_row:first_row + half]
     fl_r[me] = fl_s[me]
+    fl_source = lambda peer: fl_s.at[peer]
 
     level1.wait()
     scatter(1, mig_r[1])
@@ -292,7 +293,6 @@
             ),
         ]
 
-    fl_source = lambda peer: fl_s.at[peer]
 
     def prepare(step, blk, j):
         t = partner_features(blk).T.astype(BF16)
@@ -312,7 +312,7 @@
         flrow[...] = jnp.zeros(flrow.shape, F32)
         flrow[:, 0, :] = (st0[:, 6, :] / RADIUS_REF) ** 3
         weights_copy.wait()
-        lax.fori_loop(0, nb, deposit, 0, unroll=8)
+        lax.fori_loop(0, nb, deposit, 0, unroll=16)
         mass_s[...] = dep[:, 0, :]
         mass_r[me] = mass_s[...]
         start_all(mass_source, mass_r, mass_ss, mass_rs)
@@ -328,6 +328,19 @@
                 solid = solid + jnp.dot(oh_ref[t], piece.astype(BF16), preferred_element_type=F32)
         void_out[...] = 1.0 / (1.0 + solid)
 
+    def gather_fluid():
+        wait_all(fl_source, fl_r, fl_ss, fl_rs)
+        total = fl_r[0].astype(F32)
+        for g in range(1, bis):
+            total = total + fl_r[g].astype(F32)
+        for k in range(3):
+            flrow[:, k, :] = total[:, k * BLK:(k + 1) * BLK]
+
+    def sample(n):
+        samp[n] = lax.dot_general(
+            flrow[n].astype(BF16), w_v[n], (((1,), (1,)), ((), ())), preferred_element_type=F32
+        )
+
     def contacts(step, state):
         for copy in halo_copies(step, state):
             copy.start()
@@ -340,7 +353,7 @@
             b_ref[n] = local_features(blk)
             return 0
 
-        lax.fori_loop(0, nb, own_blocks, 0, unroll=4)
+        lax.fori_loop(0, nb, own_blocks, 0, unroll=8)
         if step == 0:
             deposit_mass()
         if step == 1:
@@ -353,7 +366,7 @@
             prepare(step, halo_r[step, n + G], n + nb + G)
             return 0
 
-        lax.fori_loop(0, G, rim, 0, unroll=2)
+        lax.fori_loop(0, G, rim, 0, unroll=4)
 
         def pair(i, _):
             a = jnp.minimum(pairs_ref[0, i], nb - 1)
@@ -369,7 +382,23 @@
             ])
             return 0
 
-        lax.fori_loop(0, pmax, pair, 0, unroll=min(32, pmax))
+        if step == 0:
+            first = pmax * 2 // 3
+            lax.fori_loop(0, first, pair, 0, unroll=min(32, first))
+            gather_fluid()
+            turns = 2
+            pairs_each, blocks_each = (pmax - first) // turns, nb // turns
+
+            def mixed(turn, _):
+                for u in range(pairs_each):
+                    pair(first + turn * pairs_each + u, 0)
+                    for v in range(blocks_each * u // pairs_each, blocks_each * (u + 1) // pairs_each):
+                        sample(turn * blocks_each + v)
+                return 0
+
+            lax.fori_loop(0, turns, mixed, 0)
+        else:
+            lax.fori_loop(0, pmax, pair, 0, unroll=min(32, pmax))
         lane = lax.broadcasted_iota(jnp.int32, (nb, pmax), 1)
         blk_id = lax.broadcasted_iota(jnp.int32, (nb, pmax), 0)
         hot = jnp.where((left_ref[0:1] == blk_id) & (lane < cnt_ref[0, 0]), 1.0, 0.0).astype(BF16)
@@ -381,28 +410,11 @@
             out.append(acc)
         return out
 
-    def sample():
-        wait_all(fl_source, fl_r, fl_ss, fl_rs)
-        total = fl_r[0].astype(F32)
-        for g in range(1, bis):
-            total = total + fl_r[g].astype(F32)
-        for k in range(3):
-            flrow[:, k, :] = total[:, k * BLK:(k + 1) * BLK]
-
-        def step(n, _):
-            samp[n] = lax.dot_general(
-                flrow[n].astype(BF16), w_v[n], (((1,), (1,)), ((), ())), preferred_element_type=F32
-            )
-            return 0
-
-        lax.fori_loop(0, nb, step, 0, unroll=8)
-
     radius, beta = None, None
     for substep in range(SUBSTEPS):
         state = (st0, st1)[substep]
         contact = contacts(substep, state)
         if substep == 0:
-            sample()
             sampled = [samp[:, k, :] for k in range(3)]
             radius, beta = st0[:, 6, :], st0[:, 7, :]
             masses = (radius / RADIUS_REF) ** 3
@@ -457,7 +469,7 @@
 
     routes = ((along_z, steps_z, along_y, steps_y), (along_y, steps_y, along_z, steps_z))
     for h in range(2):
-        lax.fori_loop(half * h, half * (h + 1), deposit, 0, unroll=8)
+        lax.fori_loop(half * h, half * (h + 1), deposit, 0, unroll=16)
         buffer = (da, db)[h]
         for k in range(3):
             buffer[me, k] = dep[half * h:half * (h + 1), k, :]
@@ -535,7 +547,7 @@
         in_specs=[hbm] * 12,
         out_specs=(hbm,) * 4,
         scratch_shapes=[
-            pltpu.SMEM((levels, capacity), jnp.int32),
+            pltpu.SMEM((levels, 1, capacity), jnp.int32),
             pltpu.SMEM((1, levels), jnp.int32),
             pltpu.SMEM((2, pmax), jnp.int32),
             pltpu.SMEM((1, 1), jnp.int32),
@@ -603,7 +615,7 @@
         jnp.transpose(velocities[0], (1, 0, 2)),
         radii[0],
         drag_rates[0],
-        mig_slots[0],
+        jnp.transpose(mig_slots, (1, 0, 2)),
         mig_counts,
         pair_lists[0],
         pair_counts,

time: 61.2 us -> 58 us (0.948)
  Pallas kernels: 58.5 us -> 56.1 us
  local copies, waits for them, and re-layouts: 1.25 us -> 0 us
    pallas_call x1, Pallas kernels: 56.7 us -> 54.4 us  [local(): pl.pallas_call(functools.partial(kernel, bis, dom, pmax), out_shape=(jax....]
    unnamed x3 -> x0, local copies, waits for them, and re-layouts: 1.25 us -> none
where the time goes in v6:
time: 58 us; the launch traced here: 57.4 us
  Pallas kernels  56.1 us (97%)
  between operations  1.29 us (2%)
    pallas_call x1, Pallas kernels, local(): pl.pallas_call(functools.partial(kernel, bis, dom, pmax), out_shape=(jax....  54.4 us
    pallas_call x1, Pallas kernels, local(): pl.pallas_call(copy_out, out_shape=tuple((jax.ShapeDtypeStruct(out.shape,...  1.75 us

profile of v6, /device:TPU:0, one launch (start us, length us, event | category | flops | bytes accessed | tf_op | source)
XLA Modules:
  0.0 57.4 jit_solution(12980181237592285525)
XLA Ops:
  1.3 54.4 %shard_map.138 = (f32[3,32,128]{2,1,0:T(8,128)}, f32[3,32,128]{2,1,0:T(8,128)}, f32[3,128,128]{2,1,0:T(8,128)}, f32[128,128]{1,0:T(8,128)}) custom-call(f32[3,32,128]{2,1,0:T(8,128)} %bitcast.26, f32[3,32,128]{2,1,0:T(8,128)} %bitcast.27, f32[32,128]{1,0:T(8,128)} %bitcast.28, f32[32,128]{1,0:T(8,128)} %bitcast.29, s32[3,1,16]{2,1,0:T(1,128)} %bitcast.32, ...), custom_call_target="tpu_custom_call" | custom-call | tf_op jit(solution)/shard_map/pallas_call | solution.py:539
  55.6 1.8 %shard_map.139 = (f32[3,32,128]{2,1,0:T(8,128)}, f32[3,32,128]{2,1,0:T(8,128)}, f32[3,128,128]{2,1,0:T(8,128)}, f32[128,128]{1,0:T(8,128)}) custom-call(f32[3,32,128]{2,1,0:T(8,128)} %get-tuple-element.12.refs_0_, f32[3,32,128]{2,1,0:T(8,128)} %get-tuple-element.13.refs_1_, f32[3,128,128]{2,1,0:T(8,128)} %get-tuple-element.14.refs_2_, ...), custom_call_target="tpu_custom_call" | custom-call | tf_op jit(solution)/shard_map/pallas_call | solution.py:627

commit v7 on v6

--- a/solution.py
+++ b/solution.py
@@ -172,7 +172,7 @@
             target[j] = st0[slots_ref[level, 0, j]]
             return 0
 
-        lax.fori_loop(0, capacity, step, 0, unroll=8)
+        lax.fori_loop(0, capacity, step, 0, unroll=16)
 
     def flip(level):
         stride = 2**level
@@ -190,7 +190,7 @@
             st0[n] = jnp.where(j >= 0, arrived[jnp.maximum(j, 0)], st0[n])
             return 0
 
-        lax.fori_loop(0, nb, step, 0, unroll=8)
+        lax.fori_loop(0, nb, step, 0, unroll=16)
 
     near, far = me + flip(1), me + flip(2)
     both = far + flip(1)
@@ -217,14 +217,14 @@
             mig_s[3][j] = block
             return 0
 
-        lax.fori_loop(0, capacity, step, 0, unroll=4)
+        lax.fori_loop(0, capacity, step, 0, unroll=16)
 
     def merge_level2():
         def step(j, _):
             mig_r[2][j] = jnp.where(from_far[pl.ds(j, 1), :] >= 0, mig_r[3][j], mig_r[2][j])
             return 0
 
-        lax.fori_loop(0, capacity, step, 0, unroll=8)
+        lax.fori_loop(0, capacity, step, 0, unroll=16)
 
     gather(0, mig_s[0])
     inv_copy.wait()
@@ -308,11 +308,12 @@
         dep[n] = jnp.dot(flrow[n].astype(BF16), w_v[n], preferred_element_type=F32)
         return 0
 
-    def deposit_mass():
+    def load_mass():
         flrow[...] = jnp.zeros(flrow.shape, F32)
         flrow[:, 0, :] = (st0[:, 6, :] / RADIUS_REF) ** 3
         weights_copy.wait()
-        lax.fori_loop(0, nb, deposit, 0, unroll=16)
+
+    def send_mass():
         mass_s[...] = dep[:, 0, :]
         mass_r[me] = mass_s[...]
         start_all(mass_source, mass_r, mass_ss, mass_rs)
@@ -336,7 +337,7 @@
         for k in range(3):
             flrow[:, k, :] = total[:, k * BLK:(k + 1) * BLK]
 
-    def sample(n):
+    def sample(n, _):
         samp[n] = lax.dot_general(
             flrow[n].astype(BF16), w_v[n], (((1,), (1,)), ((), ())), preferred_element_type=F32
         )
@@ -354,8 +355,6 @@
             return 0
 
         lax.fori_loop(0, nb, own_blocks, 0, unroll=8)
-        if step == 0:
-            deposit_mass()
         if step == 1:
             solid_volume()
         for copy in halo_copies(step, state):
@@ -382,23 +381,27 @@
             ])
             return 0
 
+        def beside(begin, end, turns, extra):
+            pairs_each, blocks_each = (end - begin) // turns, nb // turns
+
+            def mixed(turn, _):
+                for u in range(pairs_each):
+                    pair(begin + turn * pairs_each + u, 0)
+                    for v in range(blocks_each * u // pairs_each, blocks_each * (u + 1) // pairs_each):
+                        extra(turn * blocks_each + v, 0)
+                return 0
+
+            lax.fori_loop(0, turns, mixed, 0)
+
         if step == 0:
             first = pmax * 2 // 3
-            lax.fori_loop(0, first, pair, 0, unroll=min(32, first))
+            load_mass()
+            beside(0, first, 4 if first % 4 == 0 else 2, deposit)
+            send_mass()
             gather_fluid()
-            turns = 2
-            pairs_each, blocks_each = (pmax - first) // turns, nb // turns
-
-            def mixed(turn, _):
-                for u in range(pairs_each):
-                    pair(first + turn * pairs_each + u, 0)
-                    for v in range(blocks_each * u // pairs_each, blocks_each * (u + 1) // pairs_each):
-                        sample(turn * blocks_each + v)
-                return 0
-
-            lax.fori_loop(0, turns, mixed, 0)
+            beside(first, pmax, 2, sample)
         else:
-            lax.fori_loop(0, pmax, pair, 0, unroll=min(32, pmax))
+            lax.fori_loop(0, pmax, pair, 0, unroll=min(48, pmax))
         lane = lax.broadcasted_iota(jnp.int32, (nb, pmax), 1)
         blk_id = lax.broadcasted_iota(jnp.int32, (nb, pmax), 0)
         hot = jnp.where((left_ref[0:1] == blk_id) & (lane < cnt_ref[0, 0]), 1.0, 0.0).astype(BF16)

time: 58 us -> 57.2 us (0.986)
  no operation moved by 1% of the time
where the time goes in v7:
time: 57.2 us; the launch traced here: 57 us
  Pallas kernels  55.7 us (97%)
  between operations  1.29 us (2%)
    pallas_call x1, Pallas kernels, local(): pl.pallas_call(functools.partial(kernel, bis, dom, pmax), out_shape=(jax....  54 us
    pallas_call x1, Pallas kernels, local(): pl.pallas_call(copy_out, out_shape=tuple((jax.ShapeDtypeStruct(out.shape,...  1.75 us

profile of v7, /device:TPU:0, one launch (start us, length us, event | category | flops | bytes accessed | tf_op | source)
XLA Modules:
  0.0 57.0 jit_solution(7475243712464168729)
XLA Ops:
  1.3 54.0 %shard_map.138 = (f32[3,32,128]{2,1,0:T(8,128)}, f32[3,32,128]{2,1,0:T(8,128)}, f32[3,128,128]{2,1,0:T(8,128)}, f32[128,128]{1,0:T(8,128)}) custom-call(f32[3,32,128]{2,1,0:T(8,128)} %bitcast.26, f32[3,32,128]{2,1,0:T(8,128)} %bitcast.27, f32[32,128]{1,0:T(8,128)} %bitcast.28, f32[32,128]{1,0:T(8,128)} %bitcast.29, s32[3,1,16]{2,1,0:T(1,128)} %bitcast.32, ...), custom_call_target="tpu_custom_call" | custom-call | tf_op jit(solution)/shard_map/pallas_call | solution.py:542
  55.3 1.8 %shard_map.139 = (f32[3,32,128]{2,1,0:T(8,128)}, f32[3,32,128]{2,1,0:T(8,128)}, f32[3,128,128]{2,1,0:T(8,128)}, f32[128,128]{1,0:T(8,128)}) custom-call(f32[3,32,128]{2,1,0:T(8,128)} %get-tuple-element.12.refs_0_, f32[3,32,128]{2,1,0:T(8,128)} %get-tuple-element.13.refs_1_, f32[3,128,128]{2,1,0:T(8,128)} %get-tuple-element.14.refs_2_, ...), custom_call_target="tpu_custom_call" | custom-call | tf_op jit(solution)/shard_map/pallas_call | solution.py:630

commit v8 on v7

--- a/solution.py
+++ b/solution.py
@@ -405,13 +405,10 @@
         lane = lax.broadcasted_iota(jnp.int32, (nb, pmax), 1)
         blk_id = lax.broadcasted_iota(jnp.int32, (nb, pmax), 0)
         hot = jnp.where((left_ref[0:1] == blk_id) & (lane < cnt_ref[0, 0]), 1.0, 0.0).astype(BF16)
-        out = []
-        for k in range(3):
-            acc = jnp.zeros((nb, BLK), F32)
-            for piece in split(f_ref[:, k, :], 2)[::-1]:
-                acc = acc + jnp.dot(hot, piece.astype(BF16), preferred_element_type=F32)
-            out.append(acc)
-        return out
+        hi, lo = split(jnp.concatenate([f_ref[:, k, :] for k in range(3)], axis=1), 2)
+        acc = jnp.dot(hot, lo.astype(BF16), preferred_element_type=F32)
+        acc = acc + jnp.dot(hot, hi.astype(BF16), preferred_element_type=F32)
+        return [acc[:, k * BLK:(k + 1) * BLK] for k in range(3)]
 
     radius, beta = None, None
     for substep in range(SUBSTEPS):
@@ -502,8 +499,10 @@
         acc = jnp.zeros((BLK, BLK), F32)
         for t in range(tiles):
             values = jnp.concatenate([values_of(t, h).reshape(BLK // 2, BLK) for h in range(2)], axis=0)
-            for piece in split(values, 2)[::-1]:
-                acc = acc + jnp.dot(oh_ref[t], piece.astype(BF16), preferred_element_type=F32)
+            hi, lo = split(values, 2)
+            both = jnp.concatenate([hi, lo], axis=0).astype(BF16)
+            hot = jnp.concatenate([oh_ref[t], oh_ref[t]], axis=1)
+            acc = acc + jnp.dot(hot, both, preferred_element_type=F32)
         return acc
 
     void = void_out[...]

time: 57.2 us -> 56.7 us (level)
  no operation moved by 1% of the time
where the time goes in v8:
time: 56.7 us; the launch traced here: 56.5 us
  Pallas kernels  55.2 us (97%)
  between operations  1.29 us (2%)
    pallas_call x1, Pallas kernels, local(): pl.pallas_call(functools.partial(kernel, bis, dom, pmax), out_shape=(jax....  53.5 us
    pallas_call x1, Pallas kernels, local(): pl.pallas_call(copy_out, out_shape=tuple((jax.ShapeDtypeStruct(out.shape,...  1.75 us

profile of v8, /device:TPU:0, one launch (start us, length us, event | category | flops | bytes accessed | tf_op | source)
XLA Modules:
  0.0 56.5 jit_solution(13252755297736751820)
XLA Ops:
  1.3 53.5 %shard_map.138 = (f32[3,32,128]{2,1,0:T(8,128)}, f32[3,32,128]{2,1,0:T(8,128)}, f32[3,128,128]{2,1,0:T(8,128)}, f32[128,128]{1,0:T(8,128)}) custom-call(f32[3,32,128]{2,1,0:T(8,128)} %bitcast.26, f32[3,32,128]{2,1,0:T(8,128)} %bitcast.27, f32[32,128]{1,0:T(8,128)} %bitcast.28, f32[32,128]{1,0:T(8,128)} %bitcast.29, s32[3,1,16]{2,1,0:T(1,128)} %bitcast.32, ...), custom_call_target="tpu_custom_call" | custom-call | tf_op jit(solution)/shard_map/pallas_call | solution.py:541
  54.8 1.8 %shard_map.139 = (f32[3,32,128]{2,1,0:T(8,128)}, f32[3,32,128]{2,1,0:T(8,128)}, f32[3,128,128]{2,1,0:T(8,128)}, f32[128,128]{1,0:T(8,128)}) custom-call(f32[3,32,128]{2,1,0:T(8,128)} %get-tuple-element.12.refs_0_, f32[3,32,128]{2,1,0:T(8,128)} %get-tuple-element.13.refs_1_, f32[3,128,128]{2,1,0:T(8,128)} %get-tuple-element.14.refs_2_, ...), custom_call_target="tpu_custom_call" | custom-call | tf_op jit(solution)/shard_map/pallas_call | solution.py:629
